TPU v7x, 128 devices: a whole 4x4x4 slice. The times are simulated.
128 devices in a mesh: row: 8 (over y, core), col: 16 (over z, x).
Axes of the slice: x: 4, y: 4, z: 4, core: 2. Of those that a mesh axis runs over, the one named last changes fastest.
Arguments:
- volts: bfloat16 [2, 512, 16384], P(None, ('row', 'col')), may hold values from -6 to 6
- pattern: int32 [128, 128], replicated, may hold values from -1 to 254, as said below
- owner_slot: int32 [256], replicated, may hold values from 0 to 255, each once
Outputs:
- stacks: float32 [256, 4, 255], P(('row', 'col'))
Inputs may be any that keep to these rules, and one draw needn't show every extreme that they name: pattern[p, q] is either q - p + 127 or -1; it is -1 where p == q. `owner_slot`: a permutation.
All inputs are finite; a program needn't handle non-finite values.
Results may differ from a plain program's by a relative error of at most 0.0003.
Values may be sent and summed in bfloat16 or wider, within the bound.
No kernel may reach another device: no remote copies, remote signals or barrier semaphores. Data moves between devices by JAX's collectives and lax.ppermute only.
A program may use at most 64 MiB of HBM per device.

v0:
```python
import jax
import jax.numpy as jnp
from jax import lax
from jax.sharding import PartitionSpec as P

GRID_COLUMNS = 128
RPD = 1
CHAN = 2
TIME_SAMPLES = 256


def per_device(volts, pattern, owner_slot):
    row_count = lax.axis_size("row")
    col_count = lax.axis_size("col")
    device_count = row_count * col_count
    stack_count = owner_slot.shape[0]
    sep_count = 2 * GRID_COLUMNS - 1
    lane_width = 2 * GRID_COLUMNS
    grid_rows = pattern.shape[0]
    turned = lax.all_to_all(volts, ("row", "col"), split_axis=2, concat_axis=1, tiled=True)
    local_volts = turned.reshape(2, CHAN, TIME_SAMPLES, turned.shape[2])
    column_side = lax.all_gather(local_volts, "row", axis=3, tiled=True)
    pair_cols = column_side.shape[3] // GRID_COLUMNS
    column_side = column_side.reshape(2, CHAN, TIME_SAMPLES, pair_cols, GRID_COLUMNS)
    column_rot = jnp.stack([-column_side[1], column_side[0]])
    row_index = lax.axis_index("row")
    col_index = lax.axis_index("col")
    row_rows = RPD * col_count
    pattern_rows = lax.dynamic_slice_in_dim(pattern, row_index * row_rows, row_rows, 0)
    pattern_rows = pattern_rows.reshape(row_rows, row_count, col_count, RPD)
    selected = lax.dynamic_index_in_dim(pattern_rows, col_index, 2, keepdims=False)
    selected = selected.reshape(row_rows, pair_cols)
    stack_ids = jnp.arange(stack_count, dtype=jnp.int32)
    first_col = jnp.arange(GRID_COLUMNS, dtype=jnp.int32)[:, None, None]
    second_col = jnp.arange(GRID_COLUMNS, dtype=jnp.int32)[None, :, None]
    separation = jnp.arange(lane_width, dtype=jnp.int32)[None, None, :]
    fold_table = (second_col - first_col + GRID_COLUMNS - 1 == separation).astype(jnp.float32)
    highest = lax.Precision.HIGHEST
    initial = jnp.zeros((col_count, stack_count // col_count, 2 * CHAN, lane_width), jnp.float32)
    piece = lax.all_gather(local_volts, "col", axis=3, tiled=True)
    row_total = piece.shape[3] // GRID_COLUMNS

    def one_row(offset, running):
        current = lax.dynamic_slice_in_dim(piece, offset * GRID_COLUMNS, GRID_COLUMNS, 3)
        real_part = jnp.einsum(
            "xcta,xctqb->qcab", current, column_side, preferred_element_type=jnp.float32
        )
        imag_part = jnp.einsum(
            "xcta,xctqb->qcab", current, column_rot, preferred_element_type=jnp.float32
        )
        gram = jnp.stack([real_part, imag_part], axis=2)
        folded = jnp.einsum("qcpab,abs->qcps", gram, fold_table, precision=highest)
        folded = folded.reshape(1, pair_cols, 2 * CHAN, lane_width)
        keys = lax.dynamic_index_in_dim(selected, offset, 0, keepdims=False)
        grid_row = row_index * row_rows + offset
        lowest = col_index - grid_row + grid_rows - 1
        block_start = lowest // col_count
        lane = lowest % col_count
        zero = jnp.zeros((), jnp.int32)
        corner = (lane, block_start, zero, zero)
        window = lax.dynamic_slice(running, corner, (1, pair_cols, 2 * CHAN, lane_width))
        window = window + jnp.where((keys >= 0)[None, :, None, None], folded, 0.0)
        return lax.dynamic_update_slice(running, window, corner)

    by_lane = lax.fori_loop(0, row_total, one_row, initial)
    by_stack = by_lane.transpose(1, 0, 2, 3).reshape(stack_count, 2 * CHAN, lane_width)
    by_stack = by_stack[:, :, :sep_count]
    inverse = jnp.zeros((stack_count,), jnp.int32).at[owner_slot].set(stack_ids)
    partial_sums = jnp.take(by_stack, inverse, axis=0)
    slot_count = stack_count // device_count
    owned = lax.psum_scatter(partial_sums, ("row", "col"), scatter_dimension=0, tiled=True)
    device_index = lax.axis_index(("row", "col"))
    key_of = lax.dynamic_slice_in_dim(inverse, device_index * slot_count, slot_count, 0)
    pair_counts = jnp.sum(
        (pattern[None, :, :] == key_of[:, None, None]).astype(jnp.float32), axis=(1, 2)
    )
    separation_offsets = jnp.abs(jnp.arange(sep_count, dtype=jnp.float32) - (GRID_COLUMNS - 1.0))
    antenna_pairs = pair_counts[:, None] * (GRID_COLUMNS - separation_offsets)[None, :]
    stack_scale = 1.0 / jnp.sqrt(2.0 * TIME_SAMPLES * jnp.maximum(antenna_pairs, 1.0))
    return owned * stack_scale[:, None, :]


def solution(mesh):
    return jax.shard_map(
        per_device,
        mesh=mesh,
        in_specs=(P(None, ("row", "col"), None), P(), P()),
        out_specs=P(("row", "col"), None, None),
        check_vma=False,
    )
```

profile of v0, /device:TPU:1, one launch (start us, length us, event | category | flops | bytes accessed | tf_op | source)
XLA Modules:
  0.0 563.1 jit_solution(2577773901841514946)
XLA Ops:
  6.5 15.6 %copy.33 = bf16[2,4,16384]{1,0,2:T(2,128)(2,1)} copy(bf16[2,4,16384]{2,1,0:T(4,128)(2,1)} %param.5) | data formatting | bytes 524288 | tf_op args[0]
  22.1 16.2 %reshape.166 = bf16[128,2,512]{2,1,0:T(2,128)(2,1)S(1)} reshape(bf16[16384,2,4]{2,1,0:T(2,128)(2,1)} %bitcast.68) | data formatting | bytes 524288
  38.3 22.8 %all_to_all.15 = bf16[128,2,512]{2,1,0:T(2,128)(2,1)S(1)} all-to-all(bf16[128,2,512]{2,1,0:T(2,128)(2,1)S(1)} %reshape.166), channel_id=1, replica_groups=mesh['row'=8,'col'=16] {'row','col'}, dimensions={0} | all-to-all | bytes 524288 | tf_op jit(solution)/shard_map/all_to_all | solution.py:20
  61.1 19.0 %reshape.167 = bf16[16384,2,4]{2,1,0:T(2,128)(2,1)} reshape(bf16[128,2,512]{2,1,0:T(2,128)(2,1)S(1)} %all_to_all.15) | data formatting | bytes 524288
  80.1 17.4 %copy.34 = bf16[2,4,128,128]{3,1,2,0:T(4,128)(2,1)} copy(bf16[2,4,128,128]{1,0,3,2:T(2,128)(2,1)} %bitcast.67) | data formatting | bytes 524288 | tf_op jit(solution)/shard_map/all_to_all | solution.py:20
  98.8 1.6 scatter_custom_fusion
  100.4 20.7 %all-gather.5.cloned.1.call-done = bf16[2,2,256,1024]{3,2,1,0:T(8,128)(2,1)} async-done(((bf16[2,2,256,128]{3,2,1,0:T(8,128)(2,1)}), bf16[2,2,256,1024]{3,2,1,0:T(8,128)(2,1)}) %all-gather.5.cloned.1.call-update) | async-done | bytes 2097168 | tf_op jit(solution)/shard_map/all_gather | solution.py:22
  121.2 1.7 slice_negate_fusion
  123.9 1.5 pad_maximum_fusion.1
  125.4 3.0 copy.41
  128.5 4.0 copy.35
  132.4 4.0 copy.40
  136.4 44.3 %all-gather.3.cloned.1.call-done = bf16[2,2,256,2048]{3,2,1,0:T(8,128)(2,1)} async-done(((bf16[2,2,256,128]{3,2,1,0:T(8,128)(2,1)}), bf16[2,2,256,2048]{3,2,1,0:T(8,128)(2,1)}) %all-gather.3.cloned.1.call-update) | async-done | bytes 4194320 | tf_op jit(solution)/shard_map/all_gather | solution.py:40
  180.8 223.4 %while.19 = (s32[]{:T(128)}, f32[16,16,4,256]{3,0,1,2:T(8,128)S(1)}, s32[]{:T(128)}, s32[]{:T(128)}, s32[16,8]{1,0:T(8,128)S(1)}, /*index=5*/bf16[2,2,256,2048]{...) while((s32[]{:T(128)}, ...), condition=%wide.region_2.3_spmd.clone, body=%wide.region_1.2_spmd.clone.sunk | while | flops 2156412928 | bytes 31326860 | solution.py:65
  185.1 9.3 %fusion.26 = f32[8,2,2,256,1]{3,0,4,2,1:T(8,128)S(1)} fusion(s32[128,128]{1,0:T(8,128)S(1)} %get-tuple-element.505, f32[8,2,2,128,128]{4,3,0,1,2:T(8,128)S(1)} %pad_maximum_fusion.3), kind=kOutput, calls=%fused_computation.3.clone.1 | convolution fusion | flops 1619001344 | bytes 2195456 | tf_op jit(solution)/shard_map/while/body/eval_jaxpr/qcpab,abs->qcps/dot_general | solution.py:52
  199.1 9.3 %fusion.26 = f32[8,2,2,256,1]{3,0,4,2,1:T(8,128)S(1)} fusion(s32[128,128]{1,0:T(8,128)S(1)} %get-tuple-element.505, f32[8,2,2,128,128]{4,3,0,1,2:T(8,128)S(1)} %pad_maximum_fusion.3), kind=kOutput, calls=%fused_computation.3.clone.1 | convolution fusion | flops 1619001344 | bytes 2195456 | tf_op jit(solution)/shard_map/while/body/eval_jaxpr/qcpab,abs->qcps/dot_general | solution.py:52
  213.1 9.3 %fusion.26 = f32[8,2,2,256,1]{3,0,4,2,1:T(8,128)S(1)} fusion(s32[128,128]{1,0:T(8,128)S(1)} %get-tuple-element.505, f32[8,2,2,128,128]{4,3,0,1,2:T(8,128)S(1)} %pad_maximum_fusion.3), kind=kOutput, calls=%fused_computation.3.clone.1 | convolution fusion | flops 1619001344 | bytes 2195456 | tf_op jit(solution)/shard_map/while/body/eval_jaxpr/qcpab,abs->qcps/dot_general | solution.py:52
  227.0 9.3 %fusion.26 = f32[8,2,2,256,1]{3,0,4,2,1:T(8,128)S(1)} fusion(s32[128,128]{1,0:T(8,128)S(1)} %get-tuple-element.505, f32[8,2,2,128,128]{4,3,0,1,2:T(8,128)S(1)} %pad_maximum_fusion.3), kind=kOutput, calls=%fused_computation.3.clone.1 | convolution fusion | flops 1619001344 | bytes 2195456 | tf_op jit(solution)/shard_map/while/body/eval_jaxpr/qcpab,abs->qcps/dot_general | solution.py:52
  241.0 9.3 %fusion.26 = f32[8,2,2,256,1]{3,0,4,2,1:T(8,128)S(1)} fusion(s32[128,128]{1,0:T(8,128)S(1)} %get-tuple-element.505, f32[8,2,2,128,128]{4,3,0,1,2:T(8,128)S(1)} %pad_maximum_fusion.3), kind=kOutput, calls=%fused_computation.3.clone.1 | convolution fusion | flops 1619001344 | bytes 2195456 | tf_op jit(solution)/shard_map/while/body/eval_jaxpr/qcpab,abs->qcps/dot_general | solution.py:52
  254.9 9.3 %fusion.26 = f32[8,2,2,256,1]{3,0,4,2,1:T(8,128)S(1)} fusion(s32[128,128]{1,0:T(8,128)S(1)} %get-tuple-element.505, f32[8,2,2,128,128]{4,3,0,1,2:T(8,128)S(1)} %pad_maximum_fusion.3), kind=kOutput, calls=%fused_computation.3.clone.1 | convolution fusion | flops 1619001344 | bytes 2195456 | tf_op jit(solution)/shard_map/while/body/eval_jaxpr/qcpab,abs->qcps/dot_general | solution.py:52
  268.9 9.3 %fusion.26 = f32[8,2,2,256,1]{3,0,4,2,1:T(8,128)S(1)} fusion(s32[128,128]{1,0:T(8,128)S(1)} %get-tuple-element.505, f32[8,2,2,128,128]{4,3,0,1,2:T(8,128)S(1)} %pad_maximum_fusion.3), kind=kOutput, calls=%fused_computation.3.clone.1 | convolution fusion | flops 1619001344 | bytes 2195456 | tf_op jit(solution)/shard_map/while/body/eval_jaxpr/qcpab,abs->qcps/dot_general | solution.py:52
  282.9 9.3 %fusion.26 = f32[8,2,2,256,1]{3,0,4,2,1:T(8,128)S(1)} fusion(s32[128,128]{1,0:T(8,128)S(1)} %get-tuple-element.505, f32[8,2,2,128,128]{4,3,0,1,2:T(8,128)S(1)} %pad_maximum_fusion.3), kind=kOutput, calls=%fused_computation.3.clone.1 | convolution fusion | flops 1619001344 | bytes 2195456 | tf_op jit(solution)/shard_map/while/body/eval_jaxpr/qcpab,abs->qcps/dot_general | solution.py:52
  296.8 9.3 %fusion.26 = f32[8,2,2,256,1]{3,0,4,2,1:T(8,128)S(1)} fusion(s32[128,128]{1,0:T(8,128)S(1)} %get-tuple-element.505, f32[8,2,2,128,128]{4,3,0,1,2:T(8,128)S(1)} %pad_maximum_fusion.3), kind=kOutput, calls=%fused_computation.3.clone.1 | convolution fusion | flops 1619001344 | bytes 2195456 | tf_op jit(solution)/shard_map/while/body/eval_jaxpr/qcpab,abs->qcps/dot_general | solution.py:52
  310.8 9.3 %fusion.26 = f32[8,2,2,256,1]{3,0,4,2,1:T(8,128)S(1)} fusion(s32[128,128]{1,0:T(8,128)S(1)} %get-tuple-element.505, f32[8,2,2,128,128]{4,3,0,1,2:T(8,128)S(1)} %pad_maximum_fusion.3), kind=kOutput, calls=%fused_computation.3.clone.1 | convolution fusion | flops 1619001344 | bytes 2195456 | tf_op jit(solution)/shard_map/while/body/eval_jaxpr/qcpab,abs->qcps/dot_general | solution.py:52
  324.8 9.3 %fusion.26 = f32[8,2,2,256,1]{3,0,4,2,1:T(8,128)S(1)} fusion(s32[128,128]{1,0:T(8,128)S(1)} %get-tuple-element.505, f32[8,2,2,128,128]{4,3,0,1,2:T(8,128)S(1)} %pad_maximum_fusion.3), kind=kOutput, calls=%fused_computation.3.clone.1 | convolution fusion | flops 1619001344 | bytes 2195456 | tf_op jit(solution)/shard_map/while/body/eval_jaxpr/qcpab,abs->qcps/dot_general | solution.py:52
  338.7 9.3 %fusion.26 = f32[8,2,2,256,1]{3,0,4,2,1:T(8,128)S(1)} fusion(s32[128,128]{1,0:T(8,128)S(1)} %get-tuple-element.505, f32[8,2,2,128,128]{4,3,0,1,2:T(8,128)S(1)} %pad_maximum_fusion.3), kind=kOutput, calls=%fused_computation.3.clone.1 | convolution fusion | flops 1619001344 | bytes 2195456 | tf_op jit(solution)/shard_map/while/body/eval_jaxpr/qcpab,abs->qcps/dot_general | solution.py:52
  352.7 9.3 %fusion.26 = f32[8,2,2,256,1]{3,0,4,2,1:T(8,128)S(1)} fusion(s32[128,128]{1,0:T(8,128)S(1)} %get-tuple-element.505, f32[8,2,2,128,128]{4,3,0,1,2:T(8,128)S(1)} %pad_maximum_fusion.3), kind=kOutput, calls=%fused_computation.3.clone.1 | convolution fusion | flops 1619001344 | bytes 2195456 | tf_op jit(solution)/shard_map/while/body/eval_jaxpr/qcpab,abs->qcps/dot_general | solution.py:52
  366.6 9.3 %fusion.26 = f32[8,2,2,256,1]{3,0,4,2,1:T(8,128)S(1)} fusion(s32[128,128]{1,0:T(8,128)S(1)} %get-tuple-element.505, f32[8,2,2,128,128]{4,3,0,1,2:T(8,128)S(1)} %pad_maximum_fusion.3), kind=kOutput, calls=%fused_computation.3.clone.1 | convolution fusion | flops 1619001344 | bytes 2195456 | tf_op jit(solution)/shard_map/while/body/eval_jaxpr/qcpab,abs->qcps/dot_general | solution.py:52
  380.6 9.3 %fusion.26 = f32[8,2,2,256,1]{3,0,4,2,1:T(8,128)S(1)} fusion(s32[128,128]{1,0:T(8,128)S(1)} %get-tuple-element.505, f32[8,2,2,128,128]{4,3,0,1,2:T(8,128)S(1)} %pad_maximum_fusion.3), kind=kOutput, calls=%fused_computation.3.clone.1 | convolution fusion | flops 1619001344 | bytes 2195456 | tf_op jit(solution)/shard_map/while/body/eval_jaxpr/qcpab,abs->qcps/dot_general | solution.py:52
  394.6 9.3 %fusion.26 = f32[8,2,2,256,1]{3,0,4,2,1:T(8,128)S(1)} fusion(s32[128,128]{1,0:T(8,128)S(1)} %get-tuple-element.505, f32[8,2,2,128,128]{4,3,0,1,2:T(8,128)S(1)} %pad_maximum_fusion.3), kind=kOutput, calls=%fused_computation.3.clone.1 | convolution fusion | flops 1619001344 | bytes 2195456 | tf_op jit(solution)/shard_map/while/body/eval_jaxpr/qcpab,abs->qcps/dot_general | solution.py:52
  406.2 1.4 broadcast_select_fusion
  407.9 147.4 %all-reduce.3.cloned.1.call-done = f32[256,4,255]{2,1,0:T(4,128)} async-done(((f32[256,4,255]{2,1,0:T(4,128)}), f32[256,4,255]{2,1,0:T(4,128)}) %all-reduce.3.cloned.1.call-update) | async-done | bytes 1044496
  (286 shorter events, 77.5 us)
Async XLA Ops:
  6.5 114.6 %all-gather.5.cloned.1.call-start = ((), (), s32[]{:S(2)}) async-start(), calls=%async_computation.2 | async-start | bytes 2359296 | tf_op jit(solution)/shard_map/all_gather | solution.py:22
  80.1 18.3 %copy-start.3 = (s32[128,128]{1,0:T(8,128)S(1)}, s32[128,128]{1,0:T(8,128)}, u32[]{:S(2)}) copy-start(s32[128,128]{1,0:T(8,128)} %param.6) | copy-start | bytes 196612
  80.1 18.6 %copy-start.4 = (s32[256]{0:T(256)S(1)}, s32[256]{0:T(256)}, u32[]{:S(2)}) copy-start(s32[256]{0:T(256)} %param.7) | copy-start | bytes 3076
  97.6 83.1 %all-gather.3.cloned.1.call-start = ((), (), s32[]{:S(2)}) async-start(), calls=%async_computation.1 | async-start | bytes 4456448 | tf_op jit(solution)/shard_map/all_gather | solution.py:40
  98.4 456.9 %all-reduce.3.cloned.1.call-start = ((), (), s32[]{:S(2)}) async-start(), calls=%async_computation.3 | async-start | bytes 2097152
  182.9 1.6 copy-start
  185.1 9.5 %copy-start.2 = (f32[16,16,4,256]{3,0,1,2:T(8,128)S(1)}, f32[16,16,4,256]{3,0,1,2:T(8,128)}, u32[]{:S(2)}) copy-start(f32[16,16,4,256]{3,0,1,2:T(8,128)} %copy-done.1) | copy-start | bytes 3145732 | tf_op jit(solution)/shard_map/while
  196.9 1.6 copy-start
  199.1 9.5 %copy-start.2 = (f32[16,16,4,256]{3,0,1,2:T(8,128)S(1)}, f32[16,16,4,256]{3,0,1,2:T(8,128)}, u32[]{:S(2)}) copy-start(f32[16,16,4,256]{3,0,1,2:T(8,128)} %copy-done.1) | copy-start | bytes 3145732 | tf_op jit(solution)/shard_map/while
  210.9 1.6 copy-start
  213.0 9.5 %copy-start.2 = (f32[16,16,4,256]{3,0,1,2:T(8,128)S(1)}, f32[16,16,4,256]{3,0,1,2:T(8,128)}, u32[]{:S(2)}) copy-start(f32[16,16,4,256]{3,0,1,2:T(8,128)} %copy-done.1) | copy-start | bytes 3145732 | tf_op jit(solution)/shard_map/while
  224.8 1.6 copy-start
  227.0 9.5 %copy-start.2 = (f32[16,16,4,256]{3,0,1,2:T(8,128)S(1)}, f32[16,16,4,256]{3,0,1,2:T(8,128)}, u32[]{:S(2)}) copy-start(f32[16,16,4,256]{3,0,1,2:T(8,128)} %copy-done.1) | copy-start | bytes 3145732 | tf_op jit(solution)/shard_map/while
  238.8 1.6 copy-start
  241.0 9.5 %copy-start.2 = (f32[16,16,4,256]{3,0,1,2:T(8,128)S(1)}, f32[16,16,4,256]{3,0,1,2:T(8,128)}, u32[]{:S(2)}) copy-start(f32[16,16,4,256]{3,0,1,2:T(8,128)} %copy-done.1) | copy-start | bytes 3145732 | tf_op jit(solution)/shard_map/while
  252.7 1.6 copy-start
  254.9 9.5 %copy-start.2 = (f32[16,16,4,256]{3,0,1,2:T(8,128)S(1)}, f32[16,16,4,256]{3,0,1,2:T(8,128)}, u32[]{:S(2)}) copy-start(f32[16,16,4,256]{3,0,1,2:T(8,128)} %copy-done.1) | copy-start | bytes 3145732 | tf_op jit(solution)/shard_map/while
  266.7 1.6 copy-start
  268.9 9.5 %copy-start.2 = (f32[16,16,4,256]{3,0,1,2:T(8,128)S(1)}, f32[16,16,4,256]{3,0,1,2:T(8,128)}, u32[]{:S(2)}) copy-start(f32[16,16,4,256]{3,0,1,2:T(8,128)} %copy-done.1) | copy-start | bytes 3145732 | tf_op jit(solution)/shard_map/while
  280.7 1.6 copy-start
  282.9 9.5 %copy-start.2 = (f32[16,16,4,256]{3,0,1,2:T(8,128)S(1)}, f32[16,16,4,256]{3,0,1,2:T(8,128)}, u32[]{:S(2)}) copy-start(f32[16,16,4,256]{3,0,1,2:T(8,128)} %copy-done.1) | copy-start | bytes 3145732 | tf_op jit(solution)/shard_map/while
  294.6 1.6 copy-start
  296.8 9.5 %copy-start.2 = (f32[16,16,4,256]{3,0,1,2:T(8,128)S(1)}, f32[16,16,4,256]{3,0,1,2:T(8,128)}, u32[]{:S(2)}) copy-start(f32[16,16,4,256]{3,0,1,2:T(8,128)} %copy-done.1) | copy-start | bytes 3145732 | tf_op jit(solution)/shard_map/while
  308.6 1.6 copy-start
  310.8 9.5 %copy-start.2 = (f32[16,16,4,256]{3,0,1,2:T(8,128)S(1)}, f32[16,16,4,256]{3,0,1,2:T(8,128)}, u32[]{:S(2)}) copy-start(f32[16,16,4,256]{3,0,1,2:T(8,128)} %copy-done.1) | copy-start | bytes 3145732 | tf_op jit(solution)/shard_map/while
  324.7 9.5 %copy-start.2 = (f32[16,16,4,256]{3,0,1,2:T(8,128)S(1)}, f32[16,16,4,256]{3,0,1,2:T(8,128)}, u32[]{:S(2)}) copy-start(f32[16,16,4,256]{3,0,1,2:T(8,128)} %copy-done.1) | copy-start | bytes 3145732 | tf_op jit(solution)/shard_map/while
  338.7 9.5 %copy-start.2 = (f32[16,16,4,256]{3,0,1,2:T(8,128)S(1)}, f32[16,16,4,256]{3,0,1,2:T(8,128)}, u32[]{:S(2)}) copy-start(f32[16,16,4,256]{3,0,1,2:T(8,128)} %copy-done.1) | copy-start | bytes 3145732 | tf_op jit(solution)/shard_map/while
  350.5 1.6 copy-start
  352.7 9.5 %copy-start.2 = (f32[16,16,4,256]{3,0,1,2:T(8,128)S(1)}, f32[16,16,4,256]{3,0,1,2:T(8,128)}, u32[]{:S(2)}) copy-start(f32[16,16,4,256]{3,0,1,2:T(8,128)} %copy-done.1) | copy-start | bytes 3145732 | tf_op jit(solution)/shard_map/while
  366.6 9.5 %copy-start.2 = (f32[16,16,4,256]{3,0,1,2:T(8,128)S(1)}, f32[16,16,4,256]{3,0,1,2:T(8,128)}, u32[]{:S(2)}) copy-start(f32[16,16,4,256]{3,0,1,2:T(8,128)} %copy-done.1) | copy-start | bytes 3145732 | tf_op jit(solution)/shard_map/while
  380.6 9.5 %copy-start.2 = (f32[16,16,4,256]{3,0,1,2:T(8,128)S(1)}, f32[16,16,4,256]{3,0,1,2:T(8,128)}, u32[]{:S(2)}) copy-start(f32[16,16,4,256]{3,0,1,2:T(8,128)} %copy-done.1) | copy-start | bytes 3145732 | tf_op jit(solution)/shard_map/while
  394.6 9.5 %copy-start.2 = (f32[16,16,4,256]{3,0,1,2:T(8,128)S(1)}, f32[16,16,4,256]{3,0,1,2:T(8,128)}, u32[]{:S(2)}) copy-start(f32[16,16,4,256]{3,0,1,2:T(8,128)} %copy-done.1) | copy-start | bytes 3145732 | tf_op jit(solution)/shard_map/while
  (21 other events, 23.9 us)
Sparse Core Ops, SparseCore 0:
  97.7 23.3 all-gather.4
  123.3 57.3 all-gather.2
  407.7 147.5 all-reduce.2
where the time goes:
time: 566 us; the launch traced here: 563 us
  waiting for transfers between devices  213 us (38%)
  matrix products  163 us (29%)
  local copies, waits for them, and re-layouts  138 us (24%)
  blocking collectives  22.8 us (4%)
  between operations  13.3 us (2%)
  other arithmetic  9.85 us (2%)
    dot_general x16, matrix products, one_row(): folded = jnp.einsum('qcpab,abs->qcps', gram, fold_table, precision=highest)  149 us
    unnamed x4, waiting for transfers between devices  148 us
    unnamed x10, local copies, waits for them, and re-layouts  58.5 us
    all_gather x1, waiting for transfers between devices, per_device(): piece = lax.all_gather(local_volts, 'col', axis=3, tiled=True)  44.3 us
    while x96, local copies, waits for them, and re-layouts  32.4 us
    all_to_all x1, blocking collectives, per_device(): lax.all_to_all(volts, ('row', 'col'), split_axis=2, concat_axis=1, tiled=...  22.8 us
    all_gather x1, waiting for transfers between devices, per_device(): column_side = lax.all_gather(local_volts, 'row', axis=3, tiled=True)  20.7 us
    dynamic_slice x32, local copies, waits for them, and re-layouts, one_row(): lax.dynamic_slice_in_dim(piece, offset * GRID_COLUMNS, GRID_COLUMNS, 3)  17.8 us
  transfers between devices with their start and end apart: 3, of which 3 were waited for; matrix products, arithmetic and copies ran while one was open for 3% of the time, Pallas kernels for 0%

commit v1 on v0

v1 whole, which is shorter than its diff:
```python
import jax
import jax.numpy as jnp
import numpy as np
from jax import lax
from jax.experimental import pallas as pl
from jax.experimental.pallas import tpu as pltpu
from jax.sharding import PartitionSpec as P

GRID_COLUMNS = 128
CHAN = 2
TIME_SAMPLES = 256
BINS = 2 * GRID_COLUMNS
HALF = BINS // 2
F32 = jnp.float32
BF16 = jnp.bfloat16


def split_table(table):
    table = table.astype(np.float32)
    high = table.astype(jnp.bfloat16)
    low = (table - high.astype(np.float32)).astype(jnp.bfloat16)
    return np.stack([high, low])


def forward_table():
    angle = 2.0 * np.pi * np.outer(np.arange(HALF), np.arange(GRID_COLUMNS)) / BINS
    cosine, sine = np.cos(angle), np.sin(angle)
    return split_table(np.block([[cosine, sine], [-sine, cosine]]))


def inverse_table():
    lag = np.arange(BINS) - (GRID_COLUMNS - 1)
    angle = 2.0 * np.pi * np.outer(np.arange(HALF), lag) / BINS
    return split_table(np.concatenate([np.cos(angle), np.sin(angle)]) / BINS)


def dot(left, right, contract):
    return lax.dot_general(left, right, ((contract[:1], contract[1:]), ((), ())), preferred_element_type=F32)


def halves(value):
    high = value.astype(BF16)
    return high, (value - high.astype(F32)).astype(BF16)


def skew(value):
    return pltpu.roll(value, 1, 1, stride=1, stride_axis=0)


def stack_kernel(core_ref, own_ref, peer_ref, table_ref, pattern_ref, slots_ref, out_ref, rows_ref, bins_ref, mask_ref, sums_ref):
    width = GRID_COLUMNS
    lane = lax.broadcasted_iota(jnp.int32, (1, width), 1)
    sign = jnp.where((lane % 2 == 1) & (core_ref[0] == 1), -1.0, 1.0).astype(F32)
    for part in range(2):
        for place, source in ((0, own_ref), (4, peer_ref)):
            for grid_row in range(width):
                piece = source[part, :, grid_row * width:(grid_row + 1) * width].astype(F32)
                rows_ref[part, grid_row * 8 + place:grid_row * 8 + place + 4, :] = piece * sign
    for sample in range(8):
        volts = jnp.concatenate(
            [rows_ref[part, pl.ds(sample, width, stride=8), :].astype(BF16) for part in range(2)], axis=1
        )
        bins = dot(table_ref[0], volts, (1, 1)) + dot(table_ref[1], volts, (1, 1))
        bins_ref[pl.ds(sample, HALF, stride=16), :] = bins[:HALF]
        bins_ref[pl.ds(sample + 8, HALF, stride=16), :] = bins[HALF:]
    row = lax.broadcasted_iota(jnp.int32, (width, width), 0)
    column = lax.broadcasted_iota(jnp.int32, (width, width), 1)
    reverse = (row + column == width - 1).astype(F32).astype(BF16)
    valid = (pattern_ref[...] >= 0).astype(F32).astype(BF16)
    upper = column <= row
    for which in range(2):
        mask = skew(dot(reverse, valid, (1, which)))
        mask_ref[2 * which] = jnp.where(upper, mask, 0.0)
        mask_ref[2 * which + 1] = jnp.where(upper, 0.0, mask)

    def some_bins(step, carry):
        lines = []
        for pair in range(4):
            lefts, rights = [], []
            for inner in range(2):
                left = bins_ref[pl.ds(step * 128 + pair * 32 + inner * 16, 16), :]
                real, imag = left[:8], left[8:]
                right = jnp.concatenate([real - imag, real + imag], axis=0)
                left_high, left_low = halves(left)
                right_high, right_low = halves(right)
                lefts += [left_high, left_high, left_low]
                right = jnp.concatenate([right_high, right_low, right_high], axis=0)
                empty = jnp.zeros_like(right)
                rights.append(jnp.concatenate([empty, right] if inner else [right, empty], axis=1))
            turned = dot(reverse, jnp.concatenate(lefts, axis=0), (1, 1)).astype(BF16)
            both = dot(turned, jnp.concatenate(rights, axis=0), (1, 0))
            for inner in range(2):
                product = skew(both[:, inner * width:(inner + 1) * width])
                line = []
                for which in range(4):
                    total = None
                    for tile in range(16):
                        span = slice(tile * 8, tile * 8 + 8)
                        term = product[span] * mask_ref[which, span, :]
                        total = term if total is None else total + term
                    line.append(jnp.sum(total, axis=0, keepdims=True))
                lines.append(jnp.concatenate(line, axis=1))
        sums_ref[pl.ds(pl.multiple_of(step * 8, 8), 8), :] = jnp.concatenate(lines, axis=0)
        return carry

    lax.fori_loop(0, HALF // 8, some_bins, 0)
    index = lax.broadcasted_iota(jnp.int32, (4 * width, 4 * width), 0)
    slot = 2 * (index // 4) + (index // 2) % 2
    mirrored = lax.broadcasted_iota(jnp.int32, (4 * width, 4 * width), 1) >= 2 * width
    weight = jnp.where(mirrored & (index % 2 == 1), -0.5, 0.5)
    place = jnp.where(slots_ref[...] == slot, weight, 0.0).astype(BF16)
    sums_high, sums_low = halves(sums_ref[...])
    out_ref[...] = dot(place, sums_high, (1, 1)) + dot(place, sums_low, (1, 1))


def owner_kernel(device_ref, parts_ref, table_ref, pattern_ref, slots_ref, out_ref):
    device = device_ref[0]
    lane = lax.broadcasted_iota(jnp.int32, (1, BINS), 1)
    lag = lane - (GRID_COLUMNS - 1)
    lines = []
    for core in range(2):
        for chan in range(CHAN):
            total = None
            for near in range(2):
                first = ((chan * 2 + near) * 2 + core) * 16
                part = jnp.sum(parts_ref[first:first + 16], axis=0)
                total = part if total is None else total + part
            for slot in range(2):
                real, imag = total[2 * slot:2 * slot + 1], total[2 * slot + 1:2 * slot + 2]
                lines.append(jnp.concatenate([real, imag], axis=1))
                lines.append(jnp.concatenate([imag, -real], axis=1))
    high, low = halves(jnp.concatenate(lines, axis=0))
    turned = dot(high, table_ref[0], (1, 0)) + dot(low, table_ref[0], (1, 0)) + dot(high, table_ref[1], (1, 0))
    turned = turned[:8] + jnp.where(lane % 2 == 1, 1.0, -1.0) * turned[8:]
    reach = GRID_COLUMNS - jnp.abs(lag).astype(F32)
    stack = lax.broadcasted_iota(jnp.int32, (1, BINS), 1)
    for slot in range(2):
        key = jnp.sum(jnp.where(slots_ref[...] == 2 * device + slot, stack, 0), axis=1, keepdims=True)
        count = jnp.sum((pattern_ref[...] == key).astype(F32), axis=(0, 1), keepdims=True)
        scale = 1.0 / jnp.sqrt(2.0 * TIME_SAMPLES * jnp.maximum(count * reach, 1.0))
        for chan in range(CHAN):
            for part in range(2):
                line = chan * 4 + slot * 2 + part
                value = turned[line:line + 1] * scale
                out_ref[slot, 2 * chan + part:2 * chan + part + 1, :] = value[:, :BINS - 1]


def per_device(volts, pattern, owner_slot):
    width = GRID_COLUMNS
    row_index = lax.axis_index("row")
    core = (row_index % 2).reshape(1)
    device = lax.axis_index(("row", "col")).reshape(1)
    row_count = lax.axis_size("row")
    swap = [(i, i ^ 1) for i in range(row_count)]
    peer = lax.ppermute(volts, "row", swap)
    none = jnp.full((1,), -1, jnp.int32)
    low_slots, high_slots = owner_slot[:width], owner_slot[width:]
    slots = jnp.concatenate([
        none, high_slots[:width - 1],
        none, low_slots[:width - 1],
        none, low_slots[:width - 1][::-1],
        none, high_slots[:width - 1][::-1],
    ])[None]
    vmem = pl.BlockSpec(memory_space=pltpu.VMEM)
    smem = pl.BlockSpec(memory_space=pltpu.SMEM)
    partial = pl.pallas_call(
        stack_kernel,
        out_shape=jax.ShapeDtypeStruct((4 * width, HALF), F32),
        in_specs=[smem, vmem, vmem, vmem, vmem, vmem],
        out_specs=vmem,
        scratch_shapes=[
            pltpu.VMEM((2, 8 * width, width), F32),
            pltpu.VMEM((16 * HALF, width), F32),
            pltpu.VMEM((4, width, width), F32),
            pltpu.VMEM((HALF, 4 * width), F32),
        ],
        compiler_params=pltpu.CompilerParams(vmem_limit_bytes=48 * 2 ** 20),
        name="stack_kernel",
    )(core, volts, peer, jnp.asarray(forward_table()), pattern, slots)
    parts = lax.all_to_all(partial.reshape(width, 4, HALF), ("row", "col"), split_axis=0, concat_axis=0, tiled=True)
    return pl.pallas_call(
        owner_kernel,
        out_shape=jax.ShapeDtypeStruct((2, 2 * CHAN, BINS - 1), F32),
        in_specs=[smem, vmem, vmem, vmem, vmem],
        out_specs=vmem,
        compiler_params=pltpu.CompilerParams(vmem_limit_bytes=48 * 2 ** 20),
        name="owner_kernel",
    )(device, parts, jnp.asarray(inverse_table()), pattern, owner_slot[None])


def solution(mesh):
    return jax.shard_map(
        per_device,
        mesh=mesh,
        in_specs=(P(None, ("row", "col"), None), P(), P()),
        out_specs=P(("row", "col"), None, None),
        check_vma=False,
    )
```

time: 566 us -> 42.6 us (0.08)
  waiting for transfers between devices: 213 us -> 11.9 us
  matrix products: 163 us -> 0 us
  local copies, waits for them, and re-layouts: 138 us -> 3.7 us
  blocking collectives: 22.8 us -> 0 us
  Pallas kernels: 0 us -> 14.9 us
  between operations: 13.3 us -> 0.03 us
  starting transfers between devices: 0.08 us -> 11.9 us
  other arithmetic: 9.85 us -> 0 us
    dot_general x48 -> x0, matrix products: 163 us -> none  [the longest x16 149 us: one_row(): folded = jnp.einsum('qcpab,abs->qcps', gram, fold_table, precision=highest)]
    unnamed x4 -> x0, waiting for transfers between devices: 148 us -> none
    all_gather x2 -> x0, waiting for transfers between devices: 65 us -> none  [the longest x1 44.3 us: per_device(): piece = lax.all_gather(local_volts, 'col', axis=3, tiled=True)]
    unnamed x10 -> x12, local copies, waits for them, and re-layouts: 58.5 us -> 3.42 us
    while x96 -> x0, local copies, waits for them, and re-layouts: 32.4 us -> none
    all_to_all x1 -> x0, blocking collectives: 22.8 us -> none  [per_device(): lax.all_to_all(volts, ('row', 'col'), split_axis=2, concat_axis=1, tiled=...]
    dynamic_slice x51 -> x0, local copies, waits for them, and re-layouts: 18.5 us -> none  [the longest x32 17.8 us: one_row(): lax.dynamic_slice_in_dim(piece, offset * GRID_COLUMNS, GRID_COLUMNS, 3)]
    all_to_all x1 -> x0, local copies, waits for them, and re-layouts: 17.4 us -> none  [per_device(): lax.all_to_all(volts, ('row', 'col'), split_axis=2, concat_axis=1, tiled=...]
  transfers between devices with their start and end apart: 3 -> 2, of which waited for: 3 -> 2; matrix products, arithmetic and copies ran while one was open for 3% -> 1% of each run, Pallas kernels for 0% -> 0%
where the time goes in v1:
time: 42.6 us; the launch traced here: 42.3 us
  Pallas kernels  14.9 us (35%)
  starting transfers between devices  11.9 us (28%)
  waiting for transfers between devices  11.9 us (28%)
  local copies, waits for them, and re-layouts  3.7 us (9%)
    pallas_call x1, Pallas kernels, per_device(): pl.pallas_call(stack_kernel, out_shape=jax.ShapeDtypeStruct((4 * width, H...  14 us
    all_to_all x1, waiting for transfers between devices, per_device(): lax.all_to_all(partial.reshape(width, 4, HALF), ('row', 'col'), split_axi...  11.5 us
    all_to_all x1, starting transfers between devices, per_device(): lax.all_to_all(partial.reshape(width, 4, HALF), ('row', 'col'), split_axi...  10.4 us
    unnamed x12, local copies, waits for them, and re-layouts  3.42 us
    ppermute x1, starting transfers between devices, per_device(): peer = lax.ppermute(volts, 'row', swap)  1.42 us
    pallas_call x1, Pallas kernels, per_device(): pl.pallas_call(owner_kernel, out_shape=jax.ShapeDtypeStruct((2, 2 * CHAN,...  0.86 us
  transfers between devices with their start and end apart: 2, of which 2 were waited for; matrix products, arithmetic and copies ran while one was open for 1% of the time, Pallas kernels for 0%

profile of v1, /device:TPU:1, one launch (start us, length us, event | category | flops | bytes accessed | tf_op | source)
XLA Modules:
  0.0 42.3 jit_solution(16160928484264085824)
XLA Ops:
  0.0 1.4 %collective-permute-start = (bf16[2,4,16384]{2,1,0:T(4,128)(2,1)}, bf16[2,4,16384]{2,1,0:T(4,128)(2,1)S(1)}, u32[]{:S(2)}, u32[]{:S(2)}) collective-permute-start(bf16[2,4,16384]{2,1,0:T(4,128)(2,1)} %own_ref.1), channel_id=1, source_target_pairs={{0,16},{16,0},{32,48},{48,32},{64,80},{80,64},{96,112},{112,96},{1... | collective-permute-start | bytes 786440 | tf_op jit(solution)/shard_map/ppermute | solution.py:155
  1.4 0.0 copy-start.5
  1.4 0.7 %copy-done.5 = s32[256]{0:T(256)S(1)} copy-done((s32[256]{0:T(256)S(1)}, s32[256]{0:T(256)}, u32[]{:S(2)}) %copy-start.5) | copy-done | bytes 1048
  2.1 0.1 rev.6
  2.2 0.1 rev.7
  2.3 0.1 concatenate.3
  2.4 0.4 collective-permute-done.peer_ref
  2.8 0.0 copy-start.1
  2.8 0.9 %copy-done.1 = bf16[2,4,16384]{2,1,0:T(4,128)(2,1)S(1)} copy-done((bf16[2,4,16384]{2,1,0:T(4,128)(2,1)S(1)}, bf16[2,4,16384]{2,1,0:T(4,128)(2,1)}, u32[]{:S(2)}) %copy-start.1) | copy-done | bytes 262168
  3.7 0.0 copy-start.2
  3.7 0.9 %copy-done.2 = bf16[2,256,256]{2,1,0:T(8,128)(2,1)S(1)} copy-done((bf16[2,256,256]{2,1,0:T(8,128)(2,1)S(1)}, bf16[2,256,256]{2,1,0:T(8,128)(2,1)}, u32[]{:S(2)}) %copy-start.2) | copy-done | bytes 262168
  4.7 0.0 copy-start.3
  4.7 0.8 %copy-done.3 = s32[128,128]{1,0:T(8,128)S(1)} copy-done((s32[128,128]{1,0:T(8,128)S(1)}, s32[128,128]{1,0:T(8,128)}, u32[]{:S(2)}) %copy-start.3) | copy-done | bytes 65560
  5.5 14.0 %stack_kernel.1 = f32[512,128]{1,0:T(8,128)} custom-call(s32[1]{0:T(128)} %bitcast.1.core_ref, bf16[2,4,16384]{2,1,0:T(4,128)(2,1)S(1)} %copy-done.1, bf16[2,4,16384]{2,1,0:T(4,128)(2,1)S(1)} %collective-permute-done.peer_ref, bf16[2,256,256]{2,1,0:T(8,128)(2,1)S(1)} %copy-done.2, s32[128,128]{1,0:T(8,128)S(1)} %copy-done.3, s32[1,512]{1,0:T(1,128)S(1)} %bitcast.5), custom_call_target="tpu_custom_call" | custom-call | tf_op jit(solution)/shard_map/stack_kernel/pallas_call | solution.py:166
  19.5 0.0 copy-start
  19.5 0.0 copy-start.4
  19.5 10.4 %all-to-all-start = ((f32[128,4,128]{2,1,0:T(4,128)}), f32[128,4,128]{2,1,0:T(4,128)S(1)}, u32[]{:S(2)}, u32[]{:S(2)}) async-start(f32[128,4,128]{2,1,0:T(4,128)} %bitcast.3), calls=%async_computation | async-start | bytes 524288 | tf_op jit(solution)/shard_map/all_to_all | solution.py:180
  30.0 11.5 %all-to-all-done.parts_ref = f32[128,4,128]{2,1,0:T(4,128)S(1)} async-done(((f32[128,4,128]{2,1,0:T(4,128)}), f32[128,4,128]{2,1,0:T(4,128)S(1)}, u32[]{:S(2)}, u32[]{:S(2)}) %all-to-all-start) | async-done | bytes 262176 | tf_op jit(solution)/shard_map/all_to_all | solution.py:180
  41.5 0.0 copy-done
  41.5 0.0 copy-done.4
  41.5 0.9 %owner_kernel.1 = f32[2,4,255]{2,1,0:T(4,128)} custom-call(s32[1]{0:T(128)} %bitcast.device_ref, f32[128,4,128]{2,1,0:T(4,128)S(1)} %all-to-all-done.parts_ref, bf16[2,256,256]{2,1,0:T(8,128)(2,1)S(1)} %copy-done, s32[128,128]{1,0:T(8,128)S(1)} %copy-done.4, s32[1,256]{1,0:T(1,128)S(1)} %bitcast.6), custom_call_target="tpu_custom_call" | custom-call | tf_op jit(solution)/shard_map/owner_kernel/pallas_call | solution.py:181
  (1 shorter events, 0.0 us)
Async XLA Ops:
  0.0 2.8 %collective-permute-start = (bf16[2,4,16384]{2,1,0:T(4,128)(2,1)}, bf16[2,4,16384]{2,1,0:T(4,128)(2,1)S(1)}, u32[]{:S(2)}, u32[]{:S(2)}) collective-permute-start(bf16[2,4,16384]{2,1,0:T(4,128)(2,1)} %own_ref.1), channel_id=1, source_target_pairs={{0,16},{16,0},{32,48},{48,32},{64,80},{80,64},{96,112},{112,96},{1... | collective-permute-start | bytes 786440 | tf_op jit(solution)/shard_map/ppermute | solution.py:155
  1.4 0.7 %copy-start.5 = (s32[256]{0:T(256)S(1)}, s32[256]{0:T(256)}, u32[]{:S(2)}) copy-start(s32[256]{0:T(256)} %param.7) | copy-start | bytes 3076
  2.8 0.9 %copy-start.1 = (bf16[2,4,16384]{2,1,0:T(4,128)(2,1)S(1)}, bf16[2,4,16384]{2,1,0:T(4,128)(2,1)}, u32[]{:S(2)}) copy-start(bf16[2,4,16384]{2,1,0:T(4,128)(2,1)} %own_ref.1) | copy-start | bytes 786436
  3.7 0.9 %copy-start.2 = (bf16[2,256,256]{2,1,0:T(8,128)(2,1)S(1)}, bf16[2,256,256]{2,1,0:T(8,128)(2,1)}, u32[]{:S(2)}) copy-start(bf16[2,256,256]{2,1,0:T(8,128)(2,1)} %constant.30.clone.table_ref) | copy-start | bytes 786436
  4.7 0.8 %copy-start.3 = (s32[128,128]{1,0:T(8,128)S(1)}, s32[128,128]{1,0:T(8,128)}, u32[]{:S(2)}) copy-start(s32[128,128]{1,0:T(8,128)} %pattern_ref.3) | copy-start | bytes 196612
  19.5 21.9 %copy-start = (bf16[2,256,256]{2,1,0:T(8,128)(2,1)S(1)}, bf16[2,256,256]{2,1,0:T(8,128)(2,1)}, u32[]{:S(2)}) copy-start(bf16[2,256,256]{2,1,0:T(8,128)(2,1)} %constant.31.clone.table_ref) | copy-start | bytes 786436
  19.5 21.9 %copy-start.4 = (s32[128,128]{1,0:T(8,128)S(1)}, s32[128,128]{1,0:T(8,128)}, u32[]{:S(2)}) copy-start(s32[128,128]{1,0:T(8,128)} %pattern_ref.3) | copy-start | bytes 196612
  19.5 21.9 %all-to-all-start = ((f32[128,4,128]{2,1,0:T(4,128)}), f32[128,4,128]{2,1,0:T(4,128)S(1)}, u32[]{:S(2)}, u32[]{:S(2)}) async-start(f32[128,4,128]{2,1,0:T(4,128)} %bitcast.3), calls=%async_computation | async-start | bytes 524288 | tf_op jit(solution)/shard_map/all_to_all | solution.py:180

commit v2 on v1

v2 whole, which is shorter than its diff:
```python
import jax
import jax.numpy as jnp
import numpy as np
from jax import lax
from jax.experimental import pallas as pl
from jax.experimental.pallas import tpu as pltpu
from jax.sharding import PartitionSpec as P

GRID_COLUMNS = 128
CHAN = 2
TIME_SAMPLES = 256
BINS = 2 * GRID_COLUMNS
HALF = BINS // 2
F32 = jnp.float32
BF16 = jnp.bfloat16


def split_table(table):
    table = table.astype(np.float32)
    high = table.astype(jnp.bfloat16)
    low = (table - high.astype(np.float32)).astype(jnp.bfloat16)
    return np.stack([high, low])


def forward_table():
    angle = 2.0 * np.pi * np.outer(np.arange(HALF), np.arange(GRID_COLUMNS)) / BINS
    cosine, sine = np.cos(angle), np.sin(angle)
    return split_table(np.block([[cosine, sine], [-sine, cosine]]))


def inverse_table():
    lag = np.arange(BINS) - (GRID_COLUMNS - 1)
    angle = 2.0 * np.pi * np.outer(np.arange(HALF), lag) / BINS
    return split_table(np.concatenate([np.cos(angle), np.sin(angle)]) / BINS)


def dot(left, right, contract):
    return lax.dot_general(left, right, ((contract[:1], contract[1:]), ((), ())), preferred_element_type=F32)


def halves(value):
    high = value.astype(BF16)
    return high, (value - high.astype(F32)).astype(BF16)


def skew(value):
    return pltpu.roll(value, 1, 1, stride=1, stride_axis=0)


def spread(source, rows_ref, core):
    lane = lax.broadcasted_iota(jnp.int32, (1, GRID_COLUMNS), 1)
    sign = jnp.where((lane % 2 == 1) & (core == 1), -1.0, 1.0).astype(F32)
    for part in range(2):
        for grid_row in range(GRID_COLUMNS):
            piece = source[part, :, grid_row * GRID_COLUMNS:(grid_row + 1) * GRID_COLUMNS].astype(F32)
            rows_ref[part, grid_row * 4:grid_row * 4 + 4, :] = piece * sign


def transform(rows_ref, table_ref, bins_ref):
    for sample in range(4):
        volts = jnp.concatenate(
            [rows_ref[part, pl.ds(sample, GRID_COLUMNS, stride=4), :].astype(BF16) for part in range(2)], axis=1
        )
        bins = dot(table_ref[0], volts, (1, 1)) + dot(table_ref[1], volts, (1, 1))
        bins_ref[pl.ds(sample, HALF, stride=8), :] = bins[:HALF]
        bins_ref[pl.ds(sample + 4, HALF, stride=8), :] = bins[HALF:]


def reversal():
    row = lax.broadcasted_iota(jnp.int32, (GRID_COLUMNS, GRID_COLUMNS), 0)
    column = lax.broadcasted_iota(jnp.int32, (GRID_COLUMNS, GRID_COLUMNS), 1)
    return (row + column == GRID_COLUMNS - 1).astype(F32).astype(BF16)


def own_kernel(core_ref, own_hbm, table_hbm, pattern_hbm, slots_hbm, bins_ref, mask_ref, place_ref, table_ref,
               own_ref, pattern_ref, slots_ref, rows_ref, own_sem, table_sem, pattern_sem, slots_sem):
    width = GRID_COLUMNS
    slots_copy = pltpu.make_async_copy(slots_hbm, slots_ref, slots_sem)
    own_copy = pltpu.make_async_copy(own_hbm, own_ref, own_sem)
    table_copy = pltpu.make_async_copy(table_hbm, table_ref, table_sem)
    pattern_copy = pltpu.make_async_copy(pattern_hbm, pattern_ref, pattern_sem)
    slots_copy.start()
    own_copy.start()
    pattern_copy.start()
    table_copy.start()
    reverse = reversal()
    slots_copy.wait()
    order = slots_ref[...].astype(F32)
    low, high = order[:, :width], order[:, width:]
    ahead = [pltpu.roll(half, 1, 1) for half in (high, low)]
    behind = [dot(half.astype(BF16), reverse, (1, 0)) for half in (low, high)]
    first = lax.broadcasted_iota(jnp.int32, (1, width), 1) == 0
    lane_slot = jnp.concatenate([jnp.where(first, -1.0, half) for half in ahead + behind], axis=1).astype(jnp.int32)
    index = lax.broadcasted_iota(jnp.int32, (4 * width, 4 * width), 0)
    slot = 2 * (index // 4) + (index // 2) % 2
    mirrored = lax.broadcasted_iota(jnp.int32, (4 * width, 4 * width), 1) >= 2 * width
    weight = jnp.where(mirrored & (index % 2 == 1), -0.5, 0.5)
    place_ref[...] = jnp.where(lane_slot == slot, weight, 0.0).astype(BF16)
    own_copy.wait()
    spread(own_ref, rows_ref, core_ref[0])
    pattern_copy.wait()
    valid = (pattern_ref[...] >= 0).astype(F32).astype(BF16)
    row = lax.broadcasted_iota(jnp.int32, (width, width), 0)
    column = lax.broadcasted_iota(jnp.int32, (width, width), 1)
    for which in range(2):
        mask = skew(dot(reverse, valid, (1, which)))
        mask_ref[2 * which] = jnp.where(column <= row, mask, 0.0)
        mask_ref[2 * which + 1] = jnp.where(column <= row, 0.0, mask)
    table_copy.wait()
    transform(rows_ref, table_ref, bins_ref)


def stack_kernel(core_ref, peer_ref, own_bins_ref, mask_ref, place_ref, table_ref, out_ref,
                 rows_ref, peer_bins_ref, sums_ref, left_ref, right_ref, gram_ref):
    width = GRID_COLUMNS
    spread(peer_ref, rows_ref, core_ref[0])
    transform(rows_ref, table_ref, peer_bins_ref)
    reverse = reversal()
    minus = jnp.where(lax.broadcasted_iota(jnp.int32, (8, width), 0) < 4, -1.0, 1.0).astype(F32)

    def turn_bins(step):
        lefts = []
        for inner in range(8):
            first = step * 64 + inner * 8
            left, right = [], []
            for source in (own_bins_ref, peer_bins_ref):
                tile = source[first:first + 8, :]
                left.append(tile)
                right.append(tile + minus * pltpu.roll(tile, 4, 0))
            left_high, left_low = halves(jnp.concatenate(left, axis=0))
            right_high, right_low = halves(jnp.concatenate(right, axis=0))
            lefts += [left_high, left_high, left_low, left_low]
            right_ref[step * 8 + inner] = jnp.concatenate([right_high, right_low, right_high, right_low], axis=0)
        left_ref[step] = dot(reverse, jnp.concatenate(lefts, axis=0), (1, 1)).astype(BF16)

    def gram_bins(step):
        for pair in range(4):
            rights = []
            for inner in range(2):
                right = right_ref[step * 8 + pair * 2 + inner]
                empty = jnp.zeros_like(right)
                rights.append(jnp.concatenate([empty, right] if inner else [right, empty], axis=1))
            left = left_ref[step, :, pair * width:(pair + 1) * width]
            gram_ref[step * 4 + pair] = dot(left, jnp.concatenate(rights, axis=0), (1, 0))

    def sum_bins(step):
        lines = []
        for quad in range(2):
            totals = [[None] * 4 for bin in range(4)]
            for tile in range(16):
                span = slice(tile * 8, tile * 8 + 8)
                masks = [mask_ref[which, span, :] for which in range(4)]
                for bin in range(4):
                    place = step * 4 + quad * 2 + bin // 2
                    lanes = slice(bin % 2 * width, bin % 2 * width + width)
                    shift = (1 + 8 * tile) % width
                    product = pltpu.roll(gram_ref[place, span, lanes], shift, 1, stride=1, stride_axis=0)
                    for which in range(4):
                        term = product * masks[which]
                        totals[bin][which] = term if tile == 0 else totals[bin][which] + term
            for bin in range(4):
                lines.append(jnp.concatenate([jnp.sum(total, axis=0, keepdims=True) for total in totals[bin]], axis=1))
        sums_ref[step * 8:step * 8 + 8, :] = jnp.concatenate(lines, axis=0)

    steps = HALF // 8
    for step in range(steps + 2):
        if step < steps:
            turn_bins(step)
        if 1 <= step <= steps:
            gram_bins(step - 1)
        if 2 <= step:
            sum_bins(step - 2)
    sums_high, sums_low = halves(sums_ref[...])
    out_ref[...] = dot(place_ref[...], sums_high, (1, 1)) + dot(place_ref[...], sums_low, (1, 1))


def owner_kernel(device_ref, parts_ref, table_ref, pattern_ref, slots_ref, out_ref):
    device = device_ref[0]
    lane = lax.broadcasted_iota(jnp.int32, (1, BINS), 1)
    lag = lane - (GRID_COLUMNS - 1)
    lines = []
    for core in range(2):
        for chan in range(CHAN):
            total = None
            for near in range(2):
                first = ((chan * 2 + near) * 2 + core) * 16
                part = jnp.sum(parts_ref[first:first + 16], axis=0)
                total = part if total is None else total + part
            for slot in range(2):
                real, imag = total[2 * slot:2 * slot + 1], total[2 * slot + 1:2 * slot + 2]
                lines.append(jnp.concatenate([real, imag], axis=1))
                lines.append(jnp.concatenate([imag, -real], axis=1))
    high, low = halves(jnp.concatenate(lines, axis=0))
    turned = dot(high, table_ref[0], (1, 0)) + dot(low, table_ref[0], (1, 0)) + dot(high, table_ref[1], (1, 0))
    turned = turned[:8] + jnp.where(lane % 2 == 1, 1.0, -1.0) * turned[8:]
    reach = GRID_COLUMNS - jnp.abs(lag).astype(F32)
    stack = lax.broadcasted_iota(jnp.int32, (1, BINS), 1)
    for slot in range(2):
        key = jnp.sum(jnp.where(slots_ref[...] == 2 * device + slot, stack, 0), axis=1, keepdims=True)
        count = jnp.sum((pattern_ref[...] == key).astype(F32), axis=(0, 1), keepdims=True)
        scale = 1.0 / jnp.sqrt(2.0 * TIME_SAMPLES * jnp.maximum(count * reach, 1.0))
        for chan in range(CHAN):
            for part in range(2):
                line = chan * 4 + slot * 2 + part
                value = turned[line:line + 1] * scale
                out_ref[slot, 2 * chan + part:2 * chan + part + 1, :] = value[:, :BINS - 1]


def per_device(volts, pattern, owner_slot):
    width = GRID_COLUMNS
    row_index = lax.axis_index("row")
    core = (row_index % 2).reshape(1)
    device = lax.axis_index(("row", "col")).reshape(1)
    row_count = lax.axis_size("row")
    swap = [(i, i ^ 1) for i in range(row_count)]
    peer = lax.ppermute(volts, "row", swap)
    vmem = pl.BlockSpec(memory_space=pltpu.VMEM)
    smem = pl.BlockSpec(memory_space=pltpu.SMEM)
    anywhere = pl.BlockSpec(memory_space=pltpu.HBM)
    prepared = pl.pallas_call(
        own_kernel,
        out_shape=[
            jax.ShapeDtypeStruct((8 * HALF, width), F32),
            jax.ShapeDtypeStruct((4, width, width), F32),
            jax.ShapeDtypeStruct((4 * width, 4 * width), BF16),
            jax.ShapeDtypeStruct((2, BINS, BINS), BF16),
        ],
        in_specs=[smem] + [anywhere] * 4,
        out_specs=[vmem] * 4,
        scratch_shapes=[
            pltpu.VMEM(volts.shape, BF16),
            pltpu.VMEM(pattern.shape, jnp.int32),
            pltpu.VMEM((1, 2 * width), jnp.int32),
            pltpu.VMEM((2, 4 * width, width), F32),
            pltpu.SemaphoreType.DMA,
            pltpu.SemaphoreType.DMA,
            pltpu.SemaphoreType.DMA,
            pltpu.SemaphoreType.DMA,
        ],
        compiler_params=pltpu.CompilerParams(vmem_limit_bytes=16 * 2 ** 20),
        name="own_kernel",
    )(core, *[pltpu.with_memory_space_constraint(x, pltpu.HBM) for x in (volts, jnp.asarray(forward_table()), pattern, owner_slot[None])])
    partial = pl.pallas_call(
        stack_kernel,
        out_shape=jax.ShapeDtypeStruct((4 * width, HALF), F32),
        in_specs=[smem] + [vmem] * 5,
        out_specs=vmem,
        scratch_shapes=[
            pltpu.VMEM((2, 4 * width, width), F32),
            pltpu.VMEM((8 * HALF, width), F32),
            pltpu.VMEM((HALF, 4 * width), F32),
            pltpu.VMEM((HALF // 8, width, 4 * width), BF16),
            pltpu.VMEM((HALF, 64, width), BF16),
            pltpu.VMEM((HALF // 2, width, 2 * width), F32),
        ],
        compiler_params=pltpu.CompilerParams(vmem_limit_bytes=32 * 2 ** 20),
        name="stack_kernel",
    )(core, peer, *prepared)
    parts = lax.all_to_all(partial.reshape(width, 4, HALF), ("row", "col"), split_axis=0, concat_axis=0, tiled=True)
    return pl.pallas_call(
        owner_kernel,
        out_shape=jax.ShapeDtypeStruct((2, 2 * CHAN, BINS - 1), F32),
        in_specs=[smem, vmem, vmem, vmem, vmem],
        out_specs=vmem,
        compiler_params=pltpu.CompilerParams(vmem_limit_bytes=16 * 2 ** 20),
        name="owner_kernel",
    )(device, parts, jnp.asarray(inverse_table()), pattern, owner_slot[None])


def solution(mesh):
    return jax.shard_map(
        per_device,
        mesh=mesh,
        in_specs=(P(None, ("row", "col"), None), P(), P()),
        out_specs=P(("row", "col"), None, None),
        check_vma=False,
    )
```

time: 42.6 us -> 31.5 us (0.74)
  Pallas kernels: 14.9 us -> 8.16 us
  local copies, waits for them, and re-layouts: 3.7 us -> 0.01 us
  waiting for transfers between devices: 11.9 us -> 11.4 us
    pallas_call x1, Pallas kernels: 14 us -> 5.53 us  [per_device(): pl.pallas_call(stack_kernel, out_shape=jax.ShapeDtypeStruct((4 * width, H...]
    unnamed x12 -> x6, local copies, waits for them, and re-layouts: 3.42 us -> 0.01 us
    pallas_call x0 -> x1, Pallas kernels: none -> 1.77 us  [per_device(): pl.pallas_call(own_kernel, out_shape=[jax.ShapeDtypeStruct((8 * HALF, wid...]
  transfers between devices with their start and end apart: 2 -> 2, of which waited for: 2 -> 1; matrix products, arithmetic and copies ran while one was open for 1% -> 0% of each run, Pallas kernels for 0% -> 6%
where the time goes in v2:
time: 31.5 us; the launch traced here: 31.3 us
  starting transfers between devices  11.6 us (37%)
  waiting for transfers between devices  11.4 us (36%)
  Pallas kernels  8.16 us (26%)
    all_to_all x1, waiting for transfers between devices, per_device(): lax.all_to_all(partial.reshape(width, 4, HALF), ('row', 'col'), split_axi...  11.4 us
    all_to_all x1, starting transfers between devices, per_device(): lax.all_to_all(partial.reshape(width, 4, HALF), ('row', 'col'), split_axi...  10.2 us
    pallas_call x1, Pallas kernels, per_device(): pl.pallas_call(stack_kernel, out_shape=jax.ShapeDtypeStruct((4 * width, H...  5.53 us
    pallas_call x1, Pallas kernels, per_device(): pl.pallas_call(own_kernel, out_shape=[jax.ShapeDtypeStruct((8 * HALF, wid...  1.77 us
    ppermute x1, starting transfers between devices, per_device(): peer = lax.ppermute(volts, 'row', swap)  1.42 us
    pallas_call x1, Pallas kernels, per_device(): pl.pallas_call(owner_kernel, out_shape=jax.ShapeDtypeStruct((2, 2 * CHAN,...  0.86 us
  transfers between devices with their start and end apart: 2, of which 1 were waited for; matrix products, arithmetic and copies ran while one was open for 0% of the time, Pallas kernels for 6%

profile of v2, /device:TPU:1, one launch (start us, length us, event | category | flops | bytes accessed | tf_op | source)
XLA Modules:
  0.0 31.3 jit_solution(5197636021295949474)
XLA Ops:
  0.0 1.4 %collective-permute-start = (bf16[2,4,16384]{2,1,0:T(4,128)(2,1)}, bf16[2,4,16384]{2,1,0:T(4,128)(2,1)S(1)}, u32[]{:S(2)}, u32[]{:S(2)}) collective-permute-start(bf16[2,4,16384]{2,1,0:T(4,128)(2,1)} %own_hbm.1), channel_id=1, source_target_pairs={{0,16},{16,0},{32,48},{48,32},{64,80},{80,64},{96,112},{112,96},{1... | collective-permute-start | bytes 786440 | tf_op jit(solution)/shard_map/ppermute | solution.py:216
  1.4 1.8 %own_kernel.1 = (f32[1024,128]{1,0:T(8,128)S(1)}, f32[4,128,128]{2,1,0:T(8,128)S(1)}, bf16[512,512]{1,0:T(8,128)(2,1)S(1)}, bf16[2,256,256]{2,1,0:T(8,128)(2,1)S(1)}) custom-call(s32[1]{0:T(128)} %bitcast.1.core_ref, bf16[2,4,16384]{2,1,0:T(4,128)(2,1)} %own_hbm.1, bf16[2,256,256]{2,1,0:T(8,128)(2,1)} %constant.28.clone.table_hbm, s32[128,128]{1,0:T(8,128)} %pattern_ref.1, ...), custom_call_target="tpu_custom_call" | custom-call | tf_op jit(solution)/shard_map/own_kernel/pallas_call | solution.py:220
  3.2 0.0 collective-permute-done.peer_ref
  3.2 5.5 %stack_kernel.1 = f32[512,128]{1,0:T(8,128)} custom-call(s32[1]{0:T(128)} %bitcast.1.core_ref, bf16[2,4,16384]{2,1,0:T(4,128)(2,1)S(1)} %collective-permute-done.peer_ref, f32[1024,128]{1,0:T(8,128)S(1)} %get-tuple-element.9.own_bins_ref, f32[4,128,128]{2,1,0:T(8,128)S(1)} %get-tuple-element.10.mask_ref, bf16[512,512]{1,0:T(8,128)(2,1)S(1)} %get-tuple-element.11.place_ref, ...), custom_call_target="tpu_custom_call" | custom-call | tf_op jit(solution)/shard_map/stack_kernel/pallas_call | solution.py:243
  8.7 0.0 copy-start
  8.7 0.0 copy-start.1
  8.7 10.2 %all-to-all-start = ((f32[128,4,128]{2,1,0:T(4,128)}), f32[128,4,128]{2,1,0:T(4,128)S(1)}, u32[]{:S(2)}, u32[]{:S(2)}) async-start(f32[128,4,128]{2,1,0:T(4,128)} %bitcast.3), calls=%async_computation | async-start | bytes 524288 | tf_op jit(solution)/shard_map/all_to_all | solution.py:259
  19.0 0.0 copy-start.2
  19.0 11.4 %all-to-all-done.parts_ref = f32[128,4,128]{2,1,0:T(4,128)S(1)} async-done(((f32[128,4,128]{2,1,0:T(4,128)}), f32[128,4,128]{2,1,0:T(4,128)S(1)}, u32[]{:S(2)}, u32[]{:S(2)}) %all-to-all-start) | async-done | bytes 262176 | tf_op jit(solution)/shard_map/all_to_all | solution.py:259
  30.4 0.0 copy-done
  30.4 0.0 copy-done.1
  30.4 0.0 copy-done.2
  30.4 0.9 %owner_kernel.1 = f32[2,4,255]{2,1,0:T(4,128)} custom-call(s32[1]{0:T(128)} %bitcast.device_ref, f32[128,4,128]{2,1,0:T(4,128)S(1)} %all-to-all-done.parts_ref, bf16[2,256,256]{2,1,0:T(8,128)(2,1)S(1)} %copy-done, s32[128,128]{1,0:T(8,128)S(1)} %copy-done.1, s32[1,256]{1,0:T(1,128)S(1)} %bitcast.5), custom_call_target="tpu_custom_call" | custom-call | tf_op jit(solution)/shard_map/owner_kernel/pallas_call | solution.py:260
Async XLA Ops:
  0.0 3.2 %collective-permute-start = (bf16[2,4,16384]{2,1,0:T(4,128)(2,1)}, bf16[2,4,16384]{2,1,0:T(4,128)(2,1)S(1)}, u32[]{:S(2)}, u32[]{:S(2)}) collective-permute-start(bf16[2,4,16384]{2,1,0:T(4,128)(2,1)} %own_hbm.1), channel_id=1, source_target_pairs={{0,16},{16,0},{32,48},{48,32},{64,80},{80,64},{96,112},{112,96},{1... | collective-permute-start | bytes 786440 | tf_op jit(solution)/shard_map/ppermute | solution.py:216
  8.7 21.7 %copy-start = (bf16[2,256,256]{2,1,0:T(8,128)(2,1)S(1)}, bf16[2,256,256]{2,1,0:T(8,128)(2,1)}, u32[]{:S(2)}) copy-start(bf16[2,256,256]{2,1,0:T(8,128)(2,1)} %constant.29.clone.table_ref) | copy-start | bytes 786436
  8.7 21.7 %copy-start.1 = (s32[128,128]{1,0:T(8,128)S(1)}, s32[128,128]{1,0:T(8,128)}, u32[]{:S(2)}) copy-start(s32[128,128]{1,0:T(8,128)} %pattern_ref.1) | copy-start | bytes 196612
  8.7 21.7 %all-to-all-start = ((f32[128,4,128]{2,1,0:T(4,128)}), f32[128,4,128]{2,1,0:T(4,128)S(1)}, u32[]{:S(2)}, u32[]{:S(2)}) async-start(f32[128,4,128]{2,1,0:T(4,128)} %bitcast.3), calls=%async_computation | async-start | bytes 524288 | tf_op jit(solution)/shard_map/all_to_all | solution.py:259
  19.0 11.5 %copy-start.2 = (s32[256]{0:T(256)S(1)}, s32[256]{0:T(256)}, u32[]{:S(2)}) copy-start(s32[256]{0:T(256)} %param.7) | copy-start | bytes 3076

commit v3 on v2

--- a/solution.py
+++ b/solution.py
@@ -45,6 +45,9 @@
 
 def skew(value):
     return pltpu.roll(value, 1, 1, stride=1, stride_axis=0)
+
+
+BATCH = 2
 
 
 def spread(source, rows_ref, core):
@@ -72,8 +75,9 @@
     return (row + column == GRID_COLUMNS - 1).astype(F32).astype(BF16)
 
 
-def own_kernel(core_ref, own_hbm, table_hbm, pattern_hbm, slots_hbm, bins_ref, mask_ref, place_ref, table_ref,
-               own_ref, pattern_ref, slots_ref, rows_ref, own_sem, table_sem, pattern_sem, slots_sem):
+def own_kernel(core_ref, device_ref, own_hbm, table_hbm, pattern_hbm, slots_hbm, inverse_hbm,
+               bins_ref, mask_ref, place_ref, table_ref, inverse_ref, scale_ref,
+               own_ref, pattern_ref, slots_ref, rows_ref, own_sem, table_sem, pattern_sem, slots_sem, inverse_sem):
     width = GRID_COLUMNS
     slots_copy = pltpu.make_async_copy(slots_hbm, slots_ref, slots_sem)
     own_copy = pltpu.make_async_copy(own_hbm, own_ref, own_sem)
@@ -83,6 +87,8 @@
     own_copy.start()
     pattern_copy.start()
     table_copy.start()
+    inverse_copy = pltpu.make_async_copy(inverse_hbm, inverse_ref, inverse_sem)
+    inverse_copy.start()
     reverse = reversal()
     slots_copy.wait()
     order = slots_ref[...].astype(F32)
@@ -96,18 +102,23 @@
     mirrored = lax.broadcasted_iota(jnp.int32, (4 * width, 4 * width), 1) >= 2 * width
     weight = jnp.where(mirrored & (index % 2 == 1), -0.5, 0.5)
     place_ref[...] = jnp.where(lane_slot == slot, weight, 0.0).astype(BF16)
+    pattern_copy.wait()
+    valid = (pattern_ref[...] >= 0).astype(F32).astype(BF16)
+    for which in range(2):
+        mask_ref[which] = skew(dot(reverse, valid, (1, which)))
+    lag = lax.broadcasted_iota(jnp.int32, (1, BINS), 1) - (width - 1)
+    reach = width - jnp.abs(lag).astype(F32)
+    stack = lax.broadcasted_iota(jnp.int32, (1, BINS), 1)
+    for slot in range(2):
+        mine = slots_ref[...] == 2 * device_ref[0] + slot
+        key = jnp.sum(jnp.where(mine, stack, 0), axis=1, keepdims=True)
+        count = jnp.sum((pattern_ref[...] == key).astype(F32), axis=(0, 1), keepdims=True)
+        scale_ref[slot:slot + 1, :] = 1.0 / jnp.sqrt(2.0 * TIME_SAMPLES * jnp.maximum(count * reach, 1.0))
     own_copy.wait()
     spread(own_ref, rows_ref, core_ref[0])
-    pattern_copy.wait()
-    valid = (pattern_ref[...] >= 0).astype(F32).astype(BF16)
-    row = lax.broadcasted_iota(jnp.int32, (width, width), 0)
-    column = lax.broadcasted_iota(jnp.int32, (width, width), 1)
-    for which in range(2):
-        mask = skew(dot(reverse, valid, (1, which)))
-        mask_ref[2 * which] = jnp.where(column <= row, mask, 0.0)
-        mask_ref[2 * which + 1] = jnp.where(column <= row, 0.0, mask)
     table_copy.wait()
     transform(rows_ref, table_ref, bins_ref)
+    inverse_copy.wait()
 
 
 def stack_kernel(core_ref, peer_ref, own_bins_ref, mask_ref, place_ref, table_ref, out_ref,
@@ -117,6 +128,22 @@
     transform(rows_ref, table_ref, peer_bins_ref)
     reverse = reversal()
     minus = jnp.where(lax.broadcasted_iota(jnp.int32, (8, width), 0) < 4, -1.0, 1.0).astype(F32)
+
+    lane = lax.broadcasted_iota(jnp.int32, (8, width), 1)
+    sublane = lax.broadcasted_iota(jnp.int32, (8, width), 0)
+
+    def gather_rows(tiles):
+        fours = []
+        for bin in range(4):
+            near, far = tiles[bin], tiles[bin + 4]
+            crossed = jnp.where(sublane < 4, far, near)
+            fours.append(jnp.where(sublane < 4, near, far) + pltpu.roll(crossed, 4, 0))
+        twos = []
+        for bin in range(2):
+            near, far = fours[bin], fours[bin + 2]
+            twos.append(jnp.where(sublane % 4 < 2, near + pltpu.roll(near, 6, 0), far + pltpu.roll(far, 2, 0)))
+        near, far = twos
+        return jnp.where(sublane % 2 == 0, near + pltpu.roll(near, 7, 0), far + pltpu.roll(far, 1, 0))
 
     def turn_bins(step):
         lefts = []
@@ -144,23 +171,27 @@
             gram_ref[step * 4 + pair] = dot(left, jnp.concatenate(rights, axis=0), (1, 0))
 
     def sum_bins(step):
-        lines = []
-        for quad in range(2):
-            totals = [[None] * 4 for bin in range(4)]
+        totals = [[[None] * 4 for bin in range(8)] for which in range(2)]
+        for group in range(0, 8, BATCH):
             for tile in range(16):
                 span = slice(tile * 8, tile * 8 + 8)
-                masks = [mask_ref[which, span, :] for which in range(4)]
-                for bin in range(4):
-                    place = step * 4 + quad * 2 + bin // 2
+                below = lane > sublane + tile * 8
+                masks = [mask_ref[which, span, :] for which in range(2)]
+                for bin in range(group, group + BATCH):
                     lanes = slice(bin % 2 * width, bin % 2 * width + width)
                     shift = (1 + 8 * tile) % width
-                    product = pltpu.roll(gram_ref[place, span, lanes], shift, 1, stride=1, stride_axis=0)
-                    for which in range(4):
+                    product = gram_ref[step * 4 + bin // 2, span, lanes]
+                    product = pltpu.roll(product, shift, 1, stride=1, stride_axis=0)
+                    for which in range(2):
                         term = product * masks[which]
-                        totals[bin][which] = term if tile == 0 else totals[bin][which] + term
-            for bin in range(4):
-                lines.append(jnp.concatenate([jnp.sum(total, axis=0, keepdims=True) for total in totals[bin]], axis=1))
-        sums_ref[step * 8:step * 8 + 8, :] = jnp.concatenate(lines, axis=0)
+                        total, lower = totals[which][bin][:2]
+                        total = total + term if tile else term
+                        totals[which][bin] = [total, jnp.where(below, total, lower if tile else 0.0)]
+        lines = []
+        for which in range(2):
+            total, lower = [gather_rows([totals[which][bin][kind] for bin in range(8)]) for kind in range(2)]
+            lines += [total - lower, lower]
+        sums_ref[step * 8:step * 8 + 8, :] = jnp.concatenate(lines, axis=1)
 
     steps = HALF // 8
     for step in range(steps + 2):
@@ -174,10 +205,8 @@
     out_ref[...] = dot(place_ref[...], sums_high, (1, 1)) + dot(place_ref[...], sums_low, (1, 1))
 
 
-def owner_kernel(device_ref, parts_ref, table_ref, pattern_ref, slots_ref, out_ref):
-    device = device_ref[0]
+def owner_kernel(parts_ref, table_ref, scale_ref, out_ref):
     lane = lax.broadcasted_iota(jnp.int32, (1, BINS), 1)
-    lag = lane - (GRID_COLUMNS - 1)
     lines = []
     for core in range(2):
         for chan in range(CHAN):
@@ -193,12 +222,8 @@
     high, low = halves(jnp.concatenate(lines, axis=0))
     turned = dot(high, table_ref[0], (1, 0)) + dot(low, table_ref[0], (1, 0)) + dot(high, table_ref[1], (1, 0))
     turned = turned[:8] + jnp.where(lane % 2 == 1, 1.0, -1.0) * turned[8:]
-    reach = GRID_COLUMNS - jnp.abs(lag).astype(F32)
-    stack = lax.broadcasted_iota(jnp.int32, (1, BINS), 1)
     for slot in range(2):
-        key = jnp.sum(jnp.where(slots_ref[...] == 2 * device + slot, stack, 0), axis=1, keepdims=True)
-        count = jnp.sum((pattern_ref[...] == key).astype(F32), axis=(0, 1), keepdims=True)
-        scale = 1.0 / jnp.sqrt(2.0 * TIME_SAMPLES * jnp.maximum(count * reach, 1.0))
+        scale = scale_ref[slot:slot + 1, :]
         for chan in range(CHAN):
             for part in range(2):
                 line = chan * 4 + slot * 2 + part
@@ -217,16 +242,19 @@
     vmem = pl.BlockSpec(memory_space=pltpu.VMEM)
     smem = pl.BlockSpec(memory_space=pltpu.SMEM)
     anywhere = pl.BlockSpec(memory_space=pltpu.HBM)
-    prepared = pl.pallas_call(
+    operands = (volts, jnp.asarray(forward_table()), pattern, owner_slot[None], jnp.asarray(inverse_table()))
+    *prepared, inverse, scale = pl.pallas_call(
         own_kernel,
         out_shape=[
             jax.ShapeDtypeStruct((8 * HALF, width), F32),
-            jax.ShapeDtypeStruct((4, width, width), F32),
+            jax.ShapeDtypeStruct((2, width, width), F32),
             jax.ShapeDtypeStruct((4 * width, 4 * width), BF16),
             jax.ShapeDtypeStruct((2, BINS, BINS), BF16),
+            jax.ShapeDtypeStruct((2, BINS, BINS), BF16),
+            jax.ShapeDtypeStruct((2, BINS), F32),
         ],
-        in_specs=[smem] + [anywhere] * 4,
-        out_specs=[vmem] * 4,
+        in_specs=[smem] * 2 + [anywhere] * 5,
+        out_specs=[vmem] * 6,
         scratch_shapes=[
             pltpu.VMEM(volts.shape, BF16),
             pltpu.VMEM(pattern.shape, jnp.int32),
@@ -236,10 +264,11 @@
             pltpu.SemaphoreType.DMA,
             pltpu.SemaphoreType.DMA,
             pltpu.SemaphoreType.DMA,
+            pltpu.SemaphoreType.DMA,
         ],
         compiler_params=pltpu.CompilerParams(vmem_limit_bytes=16 * 2 ** 20),
         name="own_kernel",
-    )(core, *[pltpu.with_memory_space_constraint(x, pltpu.HBM) for x in (volts, jnp.asarray(forward_table()), pattern, owner_slot[None])])
+    )(core, device, *[pltpu.with_memory_space_constraint(operand, pltpu.HBM) for operand in operands])
     partial = pl.pallas_call(
         stack_kernel,
         out_shape=jax.ShapeDtypeStruct((4 * width, HALF), F32),
@@ -260,11 +289,11 @@
     return pl.pallas_call(
         owner_kernel,
         out_shape=jax.ShapeDtypeStruct((2, 2 * CHAN, BINS - 1), F32),
-        in_specs=[smem, vmem, vmem, vmem, vmem],
+        in_specs=[vmem] * 3,
         out_specs=vmem,
         compiler_params=pltpu.CompilerParams(vmem_limit_bytes=16 * 2 ** 20),
         name="owner_kernel",
-    )(device, parts, jnp.asarray(inverse_table()), pattern, owner_slot[None])
+    )(parts, inverse, scale)
 
 
 def solution(mesh):

time: 31.5 us -> 29.7 us (0.943)
  blocking collectives: 0 us -> 21.5 us
  waiting for transfers between devices: 11.4 us -> 0.01 us
  starting transfers between devices: 11.6 us -> 1.42 us
  Pallas kernels: 8.16 us -> 6.64 us
    all_to_all x0 -> x1, blocking collectives: none -> 21.5 us  [per_device(): lax.all_to_all(partial.reshape(width, 4, HALF), ('row', 'col'), split_axi...]
    all_to_all x1 -> x0, waiting for transfers between devices: 11.4 us -> none  [per_device(): lax.all_to_all(partial.reshape(width, 4, HALF), ('row', 'col'), split_axi...]
    all_to_all x1 -> x0, starting transfers between devices: 10.2 us -> none  [per_device(): lax.all_to_all(partial.reshape(width, 4, HALF), ('row', 'col'), split_axi...]
    pallas_call x1, Pallas kernels: 5.53 us -> 4.06 us  [per_device(): pl.pallas_call(stack_kernel, out_shape=jax.ShapeDtypeStruct((4 * width, H...]
  transfers between devices with their start and end apart: 2 -> 1, of which waited for: 1 -> 0; matrix products, arithmetic and copies ran while one was open for 0% -> 0% of each run, Pallas kernels for 6% -> 6%
where the time goes in v3:
time: 29.7 us; the launch traced here: 29.5 us
  blocking collectives  21.5 us (72%)
  Pallas kernels  6.64 us (22%)
  starting transfers between devices  1.42 us (5%)
    all_to_all x1, blocking collectives, per_device(): lax.all_to_all(partial.reshape(width, 4, HALF), ('row', 'col'), split_axi...  21.5 us
    pallas_call x1, Pallas kernels, per_device(): pl.pallas_call(stack_kernel, out_shape=jax.ShapeDtypeStruct((4 * width, H...  4.06 us
    pallas_call x1, Pallas kernels, per_device(): pl.pallas_call(own_kernel, out_shape=[jax.ShapeDtypeStruct((8 * HALF, wid...  1.77 us
    ppermute x1, starting transfers between devices, per_device(): peer = lax.ppermute(volts, 'row', swap)  1.42 us
    pallas_call x1, Pallas kernels, per_device(): pl.pallas_call(owner_kernel, out_shape=jax.ShapeDtypeStruct((2, 2 * CHAN,...  0.82 us
  transfers between devices with their start and end apart: 1, of which 0 were waited for; matrix products, arithmetic and copies ran while one was open for 0% of the time, Pallas kernels for 6%

profile of v3, /device:TPU:1, one launch (start us, length us, event | category | flops | bytes accessed | tf_op | source)
XLA Modules:
  0.0 29.5 jit_solution(547478375094494758)
XLA Ops:
  0.0 1.4 %collective-permute-start = (bf16[2,4,16384]{2,1,0:T(4,128)(2,1)}, bf16[2,4,16384]{2,1,0:T(4,128)(2,1)S(1)}, u32[]{:S(2)}, u32[]{:S(2)}) collective-permute-start(bf16[2,4,16384]{2,1,0:T(4,128)(2,1)} %own_hbm.1), channel_id=1, source_target_pairs={{0,16},{16,0},{32,48},{48,32},{64,80},{80,64},{96,112},{112,96},{1... | collective-permute-start | bytes 786440 | tf_op jit(solution)/shard_map/ppermute | solution.py:241
  1.4 1.8 %own_kernel.1 = (f32[1024,128]{1,0:T(8,128)S(1)}, f32[2,128,128]{2,1,0:T(8,128)S(1)}, bf16[512,512]{1,0:T(8,128)(2,1)S(1)}, bf16[2,256,256]{2,1,0:T(8,128)(2,1)S...) custom-call(s32[1]{0:T(128)} %bitcast.core_ref, s32[1]{0:T(128)} %bitcast.1.device_ref, ...), custom_call_target="tpu_custom_call" | custom-call | tf_op jit(solution)/shard_map/own_kernel/pallas_call | solution.py:246
  3.2 0.0 collective-permute-done.peer_ref
  3.2 4.1 %stack_kernel.1 = f32[512,128]{1,0:T(8,128)S(1)} custom-call(s32[1]{0:T(128)} %bitcast.core_ref, bf16[2,4,16384]{2,1,0:T(4,128)(2,1)S(1)} %collective-permute-done.peer_ref, f32[1024,128]{1,0:T(8,128)S(1)} %get-tuple-element.11.own_bins_ref, f32[2,128,128]{2,1,0:T(8,128)S(1)} %get-tuple-element.12.mask_ref, ...), custom_call_target="tpu_custom_call" | custom-call | tf_op jit(solution)/shard_map/stack_kernel/pallas_call | solution.py:272
  7.3 21.5 %all_to_all.5.parts_ref = f32[128,4,128]{2,1,0:T(4,128)S(1)} all-to-all(f32[128,4,128]{2,1,0:T(4,128)S(1)} %bitcast.4), channel_id=1, replica_groups=mesh['row'=8,'col'=16] {'row','col'}, dimensions={0} | all-to-all | bytes 524288 | tf_op jit(solution)/shard_map/all_to_all | solution.py:288
  28.7 0.8 %owner_kernel.1 = f32[2,4,255]{2,1,0:T(4,128)} custom-call(f32[128,4,128]{2,1,0:T(4,128)S(1)} %all_to_all.5.parts_ref, bf16[2,256,256]{2,1,0:T(8,128)(2,1)S(1)} %get-tuple-element.15.table_ref, f32[2,256]{1,0:T(2,128)S(1)} %get-tuple-element.16.scale_ref), custom_call_target="tpu_custom_call" | custom-call | tf_op jit(solution)/shard_map/owner_kernel/pallas_call | solution.py:289
Async XLA Ops:
  0.0 3.2 %collective-permute-start = (bf16[2,4,16384]{2,1,0:T(4,128)(2,1)}, bf16[2,4,16384]{2,1,0:T(4,128)(2,1)S(1)}, u32[]{:S(2)}, u32[]{:S(2)}) collective-permute-start(bf16[2,4,16384]{2,1,0:T(4,128)(2,1)} %own_hbm.1), channel_id=1, source_target_pairs={{0,16},{16,0},{32,48},{48,32},{64,80},{80,64},{96,112},{112,96},{1... | collective-permute-start | bytes 786440 | tf_op jit(solution)/shard_map/ppermute | solution.py:241

commit v4 on v3

v4 whole, which is shorter than its diff:
```python
import jax
import jax.numpy as jnp
import numpy as np
from jax import lax
from jax.experimental import pallas as pl
from jax.experimental.pallas import tpu as pltpu
from jax.sharding import PartitionSpec as P

GRID_COLUMNS = 128
CHAN = 2
CHUNKS = 1
TIME_SAMPLES = 256
BINS = 2 * GRID_COLUMNS
HALF = BINS // 2
F32 = jnp.float32
BF16 = jnp.bfloat16


def split_table(table):
    table = table.astype(np.float32)
    high = table.astype(jnp.bfloat16)
    low = (table - high.astype(np.float32)).astype(jnp.bfloat16)
    return np.stack([high, low])


def forward_table():
    angle = 2.0 * np.pi * np.outer(np.arange(HALF), np.arange(GRID_COLUMNS)) / BINS
    cosine, sine = np.cos(angle), np.sin(angle)
    return np.concatenate(split_table(np.concatenate([cosine, sine], axis=1)))


def inverse_table():
    lag = np.arange(BINS) - (GRID_COLUMNS - 1)
    angle = 2.0 * np.pi * np.outer(np.arange(HALF), lag) / BINS
    return split_table(np.concatenate([np.cos(angle), np.sin(angle)]) / BINS)


def dot(left, right, contract):
    return lax.dot_general(left, right, ((contract[:1], contract[1:]), ((), ())), preferred_element_type=F32)


def halves(value):
    high = value.astype(BF16)
    return high, (value - high.astype(F32)).astype(BF16)


def skew(value):
    return pltpu.roll(value, 1, 1, stride=1, stride_axis=0)


TURN = 4
LAG_TURN = 9
LAG_GRAM = 1


def spread(source, rows_ref, core, grid_rows):
    lane = lax.broadcasted_iota(jnp.int32, (1, GRID_COLUMNS), 1)
    sign = jnp.where((lane % 2 == 1) & (core == 1), -1.0, 1.0).astype(F32)
    for part in range(2):
        for grid_row in grid_rows:
            piece = source[part, :, grid_row * GRID_COLUMNS:(grid_row + 1) * GRID_COLUMNS].astype(F32)
            rows_ref[part, grid_row * 4:grid_row * 4 + 4, :] = piece * sign


def transform(rows_ref, table_ref, bins_ref):
    for sample in range(4):
        real, imag = [rows_ref[part, pl.ds(sample, GRID_COLUMNS, stride=4), :].astype(BF16) for part in range(2)]
        volts = jnp.concatenate([jnp.concatenate([real, imag], axis=1), jnp.concatenate([imag, -real], axis=1)], axis=0)
        bins = dot(table_ref[...], volts, (1, 1))
        bins = bins[:HALF] + bins[HALF:]
        bins_ref[pl.ds(sample, HALF, stride=8), :] = bins[:, :GRID_COLUMNS]
        bins_ref[pl.ds(sample + 4, HALF, stride=8), :] = bins[:, GRID_COLUMNS:]


def reversal():
    row = lax.broadcasted_iota(jnp.int32, (GRID_COLUMNS, GRID_COLUMNS), 0)
    column = lax.broadcasted_iota(jnp.int32, (GRID_COLUMNS, GRID_COLUMNS), 1)
    return (row + column == GRID_COLUMNS - 1).astype(F32).astype(BF16)


def own_kernel(core_ref, device_ref, own_hbm, table_hbm, pattern_hbm, slots_hbm,
               bins_ref, mask_ref, place_ref, table_ref, scale_ref,
               own_ref, pattern_ref, slots_ref, rows_ref, own_sem, table_sem, pattern_sem, slots_sem):
    width = GRID_COLUMNS
    chunk = width // CHUNKS
    table_copy = pltpu.make_async_copy(table_hbm, table_ref, table_sem)
    pattern_copy = pltpu.make_async_copy(pattern_hbm, pattern_ref, pattern_sem)
    slots_copy = pltpu.make_async_copy(slots_hbm, slots_ref, slots_sem)
    slots_copy.start()
    pattern_copy.start()
    own_copies = []
    for index in range(CHUNKS):
        span = (slice(None), slice(None), pl.ds(index * chunk * width, chunk * width))
        own_copies.append(pltpu.make_async_copy(own_hbm.at[span], own_ref.at[span], own_sem.at[index]))
        own_copies[-1].start()
    table_copy.start()
    reverse = reversal()
    slots_copy.wait()
    order = slots_ref[...].astype(F32)
    low, high = order[:, :width], order[:, width:]
    ahead = [pltpu.roll(half, 1, 1) for half in (high, low)]
    behind = [dot(half.astype(BF16), reverse, (1, 0)) for half in (low, high)]
    first = lax.broadcasted_iota(jnp.int32, (1, width), 1) == 0
    lane_slot = jnp.concatenate([jnp.where(first, -1.0, half) for half in ahead + behind], axis=1).astype(jnp.int32)
    index = lax.broadcasted_iota(jnp.int32, (4 * width, 4 * width), 0)
    slot = 2 * (index // 4) + (index // 2) % 2
    mirrored = lax.broadcasted_iota(jnp.int32, (4 * width, 4 * width), 1) >= 2 * width
    weight = jnp.where(mirrored & (index % 2 == 1), -0.5, 0.5)
    place_ref[...] = jnp.where(lane_slot == slot, weight, 0.0).astype(BF16)
    pattern_copy.wait()
    valid = (pattern_ref[...] >= 0).astype(F32).astype(BF16)
    for which in range(2):
        mask_ref[which] = skew(dot(reverse, valid, (1, which)))
    lag = lax.broadcasted_iota(jnp.int32, (1, BINS), 1) - (width - 1)
    reach = width - jnp.abs(lag).astype(F32)
    stack = lax.broadcasted_iota(jnp.int32, (1, BINS), 1)
    for slot in range(2):
        mine = slots_ref[...] == 2 * device_ref[0] + slot
        key = jnp.sum(jnp.where(mine, stack, 0), axis=1, keepdims=True)
        count = jnp.sum((pattern_ref[...] == key).astype(F32), axis=(0, 1), keepdims=True)
        scale_ref[slot:slot + 1, :] = 1.0 / jnp.sqrt(2.0 * TIME_SAMPLES * jnp.maximum(count * reach, 1.0))
    for index in range(CHUNKS):
        own_copies[index].wait()
        spread(own_ref, rows_ref, core_ref[0], range(index * chunk, (index + 1) * chunk))
    table_copy.wait()
    transform(rows_ref, table_ref, bins_ref)


def stack_kernel(core_ref, peer_ref, own_bins_ref, mask_ref, place_ref, table_ref, inverse_hbm, out_ref, inverse_ref,
                 inverse_sem, rows_ref, peer_bins_ref, sums_ref, left_ref, right_ref, gram_ref):
    width = GRID_COLUMNS
    inverse_copy = pltpu.make_async_copy(inverse_hbm, inverse_ref, inverse_sem)
    inverse_copy.start()
    spread(peer_ref, rows_ref, core_ref[0], range(width))
    transform(rows_ref, table_ref, peer_bins_ref)
    reverse = reversal()
    minus = jnp.where(lax.broadcasted_iota(jnp.int32, (8, width), 0) < 4, -1.0, 1.0).astype(F32)

    lane = lax.broadcasted_iota(jnp.int32, (8, width), 1)
    sublane = lax.broadcasted_iota(jnp.int32, (8, width), 0)

    def gather_rows(tiles):
        fours = []
        for bin in range(4):
            near, far = tiles[bin], tiles[bin + 4]
            crossed = jnp.where(sublane < 4, far, near)
            fours.append(jnp.where(sublane < 4, near, far) + pltpu.roll(crossed, 4, 0))
        twos = []
        for bin in range(2):
            near, far = fours[bin], fours[bin + 2]
            twos.append(jnp.where(sublane % 4 < 2, near + pltpu.roll(near, 6, 0), far + pltpu.roll(far, 2, 0)))
        near, far = twos
        return jnp.where(sublane % 2 == 0, near + pltpu.roll(near, 7, 0), far + pltpu.roll(far, 1, 0))

    def turn_pairs(first_pair):
        lefts = []
        for bin in range(first_pair * 2, first_pair * 2 + TURN * 2):
            left, right = [], []
            for source in (own_bins_ref, peer_bins_ref):
                tile = source[bin * 8:bin * 8 + 8, :]
                left.append(tile)
                right.append(tile + minus * pltpu.roll(tile, 4, 0))
            left_high, left_low = halves(jnp.concatenate(left, axis=0))
            right_high, right_low = halves(jnp.concatenate(right, axis=0))
            lefts += [left_high, left_high, left_low, left_low]
            right_ref[bin] = jnp.concatenate([right_high, right_low, right_high, right_low], axis=0)
        turned = dot(reverse, jnp.concatenate(lefts, axis=0), (1, 1)).astype(BF16)
        for pair in range(TURN):
            left_ref[first_pair + pair] = turned[:, pair * width:(pair + 1) * width]

    def gram_pair(pair):
        rights = []
        for inner in range(2):
            right = right_ref[pair * 2 + inner]
            empty = jnp.zeros_like(right)
            rights.append(jnp.concatenate([empty, right] if inner else [right, empty], axis=1))
        left = left_ref[pair]
        gram_ref[pair] = dot(left, jnp.concatenate(rights, axis=0), (1, 0))

    def sum_pair(pair):
        totals = [[[None] * 2 for inner in range(2)] for which in range(2)]
        for tile in range(16):
            span = slice(tile * 8, tile * 8 + 8)
            below = lane > sublane + tile * 8
            for inner in range(2):
                product = gram_ref[pair, span, inner * width:(inner + 1) * width]
                product = pltpu.roll(product, (1 + 8 * tile) % width, 1, stride=1, stride_axis=0)
                for which in range(2):
                    term = product * mask_ref[which, span, :]
                    total, lower = totals[which][inner]
                    total = total + term if tile else term
                    totals[which][inner] = [total, jnp.where(below, total, lower if tile else 0.0)]
        return totals

    pairs = HALF // 2
    held = []
    for pair in range(-LAG_TURN, pairs + LAG_GRAM):
        if (pair + LAG_TURN) % TURN == 0 and pair + LAG_TURN < pairs:
            turn_pairs(pair + LAG_TURN)
        if 0 <= pair < pairs:
            gram_pair(pair)
        if 0 <= pair - LAG_GRAM:
            held.append(sum_pair(pair - LAG_GRAM))
        if len(held) == 4:
            step = (pair - LAG_GRAM) // 4
            lines = []
            for which in range(2):
                total, lower = [
                    gather_rows([held[bin // 2][which][bin % 2][kind] for bin in range(8)]) for kind in range(2)
                ]
                lines += [total - lower, lower]
            sums_ref[step * 8:step * 8 + 8, :] = jnp.concatenate(lines, axis=1)
            held = []
    both = dot(place_ref[...], jnp.concatenate(halves(sums_ref[...]), axis=0), (1, 1))
    out_ref[...] = both[:, :HALF] + both[:, HALF:]
    inverse_copy.wait()


def owner_kernel(parts_ref, table_ref, scale_ref, out_ref):
    lane = lax.broadcasted_iota(jnp.int32, (1, BINS), 1)
    lines = []
    for core in range(2):
        for chan in range(CHAN):
            total = None
            for near in range(2):
                first = ((chan * 2 + near) * 2 + core) * 16
                part = jnp.sum(parts_ref[first:first + 16], axis=0)
                total = part if total is None else total + part
            for slot in range(2):
                real, imag = total[2 * slot:2 * slot + 1], total[2 * slot + 1:2 * slot + 2]
                lines.append(jnp.concatenate([real, imag], axis=1))
                lines.append(jnp.concatenate([imag, -real], axis=1))
    high, low = halves(jnp.concatenate(lines, axis=0))
    turned = dot(high, table_ref[0], (1, 0)) + dot(low, table_ref[0], (1, 0)) + dot(high, table_ref[1], (1, 0))
    turned = turned[:8] + jnp.where(lane % 2 == 1, 1.0, -1.0) * turned[8:]
    for slot in range(2):
        scale = scale_ref[slot:slot + 1, :]
        for chan in range(CHAN):
            for part in range(2):
                line = chan * 4 + slot * 2 + part
                value = turned[line:line + 1] * scale
                out_ref[slot, 2 * chan + part:2 * chan + part + 1, :] = value[:, :BINS - 1]


def per_device(volts, pattern, owner_slot):
    width = GRID_COLUMNS
    row_index = lax.axis_index("row")
    core = (row_index % 2).reshape(1)
    device = lax.axis_index(("row", "col")).reshape(1)
    row_count = lax.axis_size("row")
    swap = [(i, i ^ 1) for i in range(row_count)]
    peer = lax.ppermute(volts, "row", swap)
    vmem = pl.BlockSpec(memory_space=pltpu.VMEM)
    smem = pl.BlockSpec(memory_space=pltpu.SMEM)
    anywhere = pl.BlockSpec(memory_space=pltpu.HBM)
    operands = (volts, jnp.asarray(forward_table()), pattern, owner_slot[None])
    *prepared, scale = pl.pallas_call(
        own_kernel,
        out_shape=[
            jax.ShapeDtypeStruct((8 * HALF, width), F32),
            jax.ShapeDtypeStruct((2, width, width), F32),
            jax.ShapeDtypeStruct((4 * width, 4 * width), BF16),
            jax.ShapeDtypeStruct((BINS, BINS), BF16),
            jax.ShapeDtypeStruct((2, BINS), F32),
        ],
        in_specs=[smem] * 2 + [anywhere] * 4,
        out_specs=[vmem] * 5,
        scratch_shapes=[
            pltpu.VMEM(volts.shape, BF16),
            pltpu.VMEM(pattern.shape, jnp.int32),
            pltpu.VMEM((1, 2 * width), jnp.int32),
            pltpu.VMEM((2, 4 * width, width), F32),
            pltpu.SemaphoreType.DMA((CHUNKS,)),
            pltpu.SemaphoreType.DMA,
            pltpu.SemaphoreType.DMA,
            pltpu.SemaphoreType.DMA,
        ],
        compiler_params=pltpu.CompilerParams(vmem_limit_bytes=16 * 2 ** 20),
        name="own_kernel",
    )(core, device, *[pltpu.with_memory_space_constraint(operand, pltpu.HBM) for operand in operands])
    partial, inverse = pl.pallas_call(
        stack_kernel,
        out_shape=[jax.ShapeDtypeStruct((4 * width, HALF), F32), jax.ShapeDtypeStruct((2, BINS, BINS), BF16)],
        in_specs=[smem] + [vmem] * 5 + [anywhere],
        out_specs=[vmem] * 2,
        scratch_shapes=[
            pltpu.SemaphoreType.DMA,
            pltpu.VMEM((2, 4 * width, width), F32),
            pltpu.VMEM((8 * HALF, width), F32),
            pltpu.VMEM((HALF, 4 * width), F32),
            pltpu.VMEM((HALF // 2, width, width), BF16),
            pltpu.VMEM((HALF, 64, width), BF16),
            pltpu.VMEM((HALF // 2, width, 2 * width), F32),
        ],
        compiler_params=pltpu.CompilerParams(vmem_limit_bytes=32 * 2 ** 20),
        name="stack_kernel",
    )(core, peer, *prepared, pltpu.with_memory_space_constraint(jnp.asarray(inverse_table()), pltpu.HBM))
    parts = lax.all_to_all(partial.reshape(width, 4, HALF), ("row", "col"), split_axis=0, concat_axis=0, tiled=True)
    return pl.pallas_call(
        owner_kernel,
        out_shape=jax.ShapeDtypeStruct((2, 2 * CHAN, BINS - 1), F32),
        in_specs=[vmem] * 3,
        out_specs=vmem,
        compiler_params=pltpu.CompilerParams(vmem_limit_bytes=16 * 2 ** 20),
        name="owner_kernel",
    )(parts, inverse, scale)


def solution(mesh):
    return jax.shard_map(
        per_device,
        mesh=mesh,
        in_specs=(P(None, ("row", "col"), None), P(), P()),
        out_specs=P(("row", "col"), None, None),
        check_vma=False,
    )
```

time: 29.7 us -> 29.3 us (0.987)
  Pallas kernels: 6.64 us -> 6.25 us
where the time goes in v4:
time: 29.3 us; the launch traced here: 29.2 us
  blocking collectives  21.5 us (73%)
  Pallas kernels  6.25 us (21%)
  starting transfers between devices  1.42 us (5%)
    all_to_all x1, blocking collectives, per_device(): lax.all_to_all(partial.reshape(width, 4, HALF), ('row', 'col'), split_axi...  21.5 us
    pallas_call x1, Pallas kernels, per_device(): pl.pallas_call(stack_kernel, out_shape=[jax.ShapeDtypeStruct((4 * width,...  3.79 us
    pallas_call x1, Pallas kernels, per_device(): pl.pallas_call(own_kernel, out_shape=[jax.ShapeDtypeStruct((8 * HALF, wid...  1.64 us
    ppermute x1, starting transfers between devices, per_device(): peer = lax.ppermute(volts, 'row', swap)  1.42 us
    pallas_call x1, Pallas kernels, per_device(): pl.pallas_call(owner_kernel, out_shape=jax.ShapeDtypeStruct((2, 2 * CHAN,...  0.82 us
  transfers between devices with their start and end apart: 1, of which 0 were waited for; matrix products, arithmetic and copies ran while one was open for 0% of the time, Pallas kernels for 6%

profile of v4, /device:TPU:1, one launch (start us, length us, event | category | flops | bytes accessed | tf_op | source)
XLA Modules:
  0.0 29.2 jit_solution(15875251314336818417)
XLA Ops:
  0.0 1.4 %collective-permute-start = (bf16[2,4,16384]{2,1,0:T(4,128)(2,1)}, bf16[2,4,16384]{2,1,0:T(4,128)(2,1)S(1)}, u32[]{:S(2)}, u32[]{:S(2)}) collective-permute-start(bf16[2,4,16384]{2,1,0:T(4,128)(2,1)} %own_hbm.1), channel_id=1, source_target_pairs={{0,16},{16,0},{32,48},{48,32},{64,80},{80,64},{96,112},{112,96},{1... | collective-permute-start | bytes 786440 | tf_op jit(solution)/shard_map/ppermute | solution.py:252
  1.4 1.6 %own_kernel.1 = (f32[1024,128]{1,0:T(8,128)S(1)}, f32[2,128,128]{2,1,0:T(8,128)S(1)}, bf16[512,512]{1,0:T(8,128)(2,1)S(1)}, bf16[256,256]{1,0:T(8,128)(2,1)S(1)}, f32[2,256]{1,0:T(2,128)S(1)}) custom-call(s32[1]{0:T(128)} %bitcast.core_ref, s32[1]{0:T(128)} %bitcast.1.device_ref, bf16[2,4,16384]{2,1,0:T(4,128)(2,1)} %own_hbm.1, ...), custom_call_target="tpu_custom_call" | custom-call | tf_op jit(solution)/shard_map/own_kernel/pallas_call | solution.py:257
  3.1 0.0 collective-permute-done.peer_ref
  3.1 3.8 %stack_kernel.1 = (f32[512,128]{1,0:T(8,128)S(1)}, bf16[2,256,256]{2,1,0:T(8,128)(2,1)S(1)}) custom-call(s32[1]{0:T(128)} %bitcast.core_ref, bf16[2,4,16384]{2,1,0:T(4,128)(2,1)S(1)} %collective-permute-done.peer_ref, f32[1024,128]{1,0:T(8,128)S(1)} %get-tuple-element.12.own_bins_ref, f32[2,128,128]{2,1,0:T(8,128)S(1)} %get-tuple-element.13.mask_ref, ...), custom_call_target="tpu_custom_call" | custom-call | tf_op jit(solution)/shard_map/stack_kernel/pallas_call | solution.py:281
  6.9 21.5 %all_to_all.5.parts_ref = f32[128,4,128]{2,1,0:T(4,128)S(1)} all-to-all(f32[128,4,128]{2,1,0:T(4,128)S(1)} %bitcast.4), channel_id=1, replica_groups=mesh['row'=8,'col'=16] {'row','col'}, dimensions={0} | all-to-all | bytes 524288 | tf_op jit(solution)/shard_map/all_to_all | solution.py:298
  28.4 0.8 %owner_kernel.1 = f32[2,4,255]{2,1,0:T(4,128)} custom-call(f32[128,4,128]{2,1,0:T(4,128)S(1)} %all_to_all.5.parts_ref, bf16[2,256,256]{2,1,0:T(8,128)(2,1)S(1)} %get-tuple-element.17.table_ref, f32[2,256]{1,0:T(2,128)S(1)} %get-tuple-element.18.scale_ref), custom_call_target="tpu_custom_call" | custom-call | tf_op jit(solution)/shard_map/owner_kernel/pallas_call | solution.py:299
Async XLA Ops:
  0.0 3.1 %collective-permute-start = (bf16[2,4,16384]{2,1,0:T(4,128)(2,1)}, bf16[2,4,16384]{2,1,0:T(4,128)(2,1)S(1)}, u32[]{:S(2)}, u32[]{:S(2)}) collective-permute-start(bf16[2,4,16384]{2,1,0:T(4,128)(2,1)} %own_hbm.1), channel_id=1, source_target_pairs={{0,16},{16,0},{32,48},{48,32},{64,80},{80,64},{96,112},{112,96},{1... | collective-permute-start | bytes 786440 | tf_op jit(solution)/shard_map/ppermute | solution.py:252

commit v5 on v4

--- a/solution.py
+++ b/solution.py
@@ -8,7 +8,6 @@
 
 GRID_COLUMNS = 128
 CHAN = 2
-CHUNKS = 1
 TIME_SAMPLES = 256
 BINS = 2 * GRID_COLUMNS
 HALF = BINS // 2
@@ -26,7 +25,9 @@
 def forward_table():
     angle = 2.0 * np.pi * np.outer(np.arange(HALF), np.arange(GRID_COLUMNS)) / BINS
     cosine, sine = np.cos(angle), np.sin(angle)
-    return np.concatenate(split_table(np.concatenate([cosine, sine], axis=1)))
+    table = np.concatenate([cosine, sine], axis=1)
+    tables = [np.concatenate(split_table(table * sign)) for sign in (1.0, np.tile([1.0, -1.0], GRID_COLUMNS))]
+    return np.stack(tables)
 
 
 def inverse_table():
@@ -48,18 +49,16 @@
     return pltpu.roll(value, 1, 1, stride=1, stride_axis=0)
 
 
-TURN = 4
-LAG_TURN = 9
+TURN = 2
+LAG_TURN = 10
 LAG_GRAM = 1
 
 
-def spread(source, rows_ref, core, grid_rows):
-    lane = lax.broadcasted_iota(jnp.int32, (1, GRID_COLUMNS), 1)
-    sign = jnp.where((lane % 2 == 1) & (core == 1), -1.0, 1.0).astype(F32)
+def spread(source, rows_ref):
     for part in range(2):
-        for grid_row in grid_rows:
-            piece = source[part, :, grid_row * GRID_COLUMNS:(grid_row + 1) * GRID_COLUMNS].astype(F32)
-            rows_ref[part, grid_row * 4:grid_row * 4 + 4, :] = piece * sign
+        for grid_row in range(GRID_COLUMNS):
+            piece = source[part, :, grid_row * GRID_COLUMNS:(grid_row + 1) * GRID_COLUMNS]
+            rows_ref[part, grid_row * 4:grid_row * 4 + 4, :] = piece.astype(F32)
 
 
 def transform(rows_ref, table_ref, bins_ref):
@@ -82,17 +81,13 @@
                bins_ref, mask_ref, place_ref, table_ref, scale_ref,
                own_ref, pattern_ref, slots_ref, rows_ref, own_sem, table_sem, pattern_sem, slots_sem):
     width = GRID_COLUMNS
-    chunk = width // CHUNKS
-    table_copy = pltpu.make_async_copy(table_hbm, table_ref, table_sem)
+    table_copy = pltpu.make_async_copy(table_hbm.at[core_ref[0]], table_ref, table_sem)
     pattern_copy = pltpu.make_async_copy(pattern_hbm, pattern_ref, pattern_sem)
     slots_copy = pltpu.make_async_copy(slots_hbm, slots_ref, slots_sem)
     slots_copy.start()
     pattern_copy.start()
-    own_copies = []
-    for index in range(CHUNKS):
-        span = (slice(None), slice(None), pl.ds(index * chunk * width, chunk * width))
-        own_copies.append(pltpu.make_async_copy(own_hbm.at[span], own_ref.at[span], own_sem.at[index]))
-        own_copies[-1].start()
+    own_copy = pltpu.make_async_copy(own_hbm, own_ref, own_sem)
+    own_copy.start()
     table_copy.start()
     reverse = reversal()
     slots_copy.wait()
@@ -119,25 +114,25 @@
         key = jnp.sum(jnp.where(mine, stack, 0), axis=1, keepdims=True)
         count = jnp.sum((pattern_ref[...] == key).astype(F32), axis=(0, 1), keepdims=True)
         scale_ref[slot:slot + 1, :] = 1.0 / jnp.sqrt(2.0 * TIME_SAMPLES * jnp.maximum(count * reach, 1.0))
-    for index in range(CHUNKS):
-        own_copies[index].wait()
-        spread(own_ref, rows_ref, core_ref[0], range(index * chunk, (index + 1) * chunk))
+    own_copy.wait()
+    spread(own_ref, rows_ref)
     table_copy.wait()
     transform(rows_ref, table_ref, bins_ref)
 
 
-def stack_kernel(core_ref, peer_ref, own_bins_ref, mask_ref, place_ref, table_ref, inverse_hbm, out_ref, inverse_ref,
+def stack_kernel(peer_ref, own_bins_ref, mask_ref, place_ref, table_ref, inverse_hbm, out_ref, inverse_ref,
                  inverse_sem, rows_ref, peer_bins_ref, sums_ref, left_ref, right_ref, gram_ref):
     width = GRID_COLUMNS
     inverse_copy = pltpu.make_async_copy(inverse_hbm, inverse_ref, inverse_sem)
     inverse_copy.start()
-    spread(peer_ref, rows_ref, core_ref[0], range(width))
+    spread(peer_ref, rows_ref)
     transform(rows_ref, table_ref, peer_bins_ref)
     reverse = reversal()
     minus = jnp.where(lax.broadcasted_iota(jnp.int32, (8, width), 0) < 4, -1.0, 1.0).astype(F32)
 
     lane = lax.broadcasted_iota(jnp.int32, (8, width), 1)
     sublane = lax.broadcasted_iota(jnp.int32, (8, width), 0)
+    offset = lane - sublane
 
     def gather_rows(tiles):
         fours = []
@@ -181,7 +176,7 @@
         totals = [[[None] * 2 for inner in range(2)] for which in range(2)]
         for tile in range(16):
             span = slice(tile * 8, tile * 8 + 8)
-            below = lane > sublane + tile * 8
+            below = offset > tile * 8
             for inner in range(2):
                 product = gram_ref[pair, span, inner * width:(inner + 1) * width]
                 product = pltpu.roll(product, (1 + 8 * tile) % width, 1, stride=1, stride_axis=0)
@@ -270,7 +265,7 @@
             pltpu.VMEM(pattern.shape, jnp.int32),
             pltpu.VMEM((1, 2 * width), jnp.int32),
             pltpu.VMEM((2, 4 * width, width), F32),
-            pltpu.SemaphoreType.DMA((CHUNKS,)),
+            pltpu.SemaphoreType.DMA,
             pltpu.SemaphoreType.DMA,
             pltpu.SemaphoreType.DMA,
             pltpu.SemaphoreType.DMA,
@@ -281,7 +276,7 @@
     partial, inverse = pl.pallas_call(
         stack_kernel,
         out_shape=[jax.ShapeDtypeStruct((4 * width, HALF), F32), jax.ShapeDtypeStruct((2, BINS, BINS), BF16)],
-        in_specs=[smem] + [vmem] * 5 + [anywhere],
+        in_specs=[vmem] * 5 + [anywhere],
         out_specs=[vmem] * 2,
         scratch_shapes=[
             pltpu.SemaphoreType.DMA,
@@ -294,7 +289,7 @@
         ],
         compiler_params=pltpu.CompilerParams(vmem_limit_bytes=32 * 2 ** 20),
         name="stack_kernel",
-    )(core, peer, *prepared, pltpu.with_memory_space_constraint(jnp.asarray(inverse_table()), pltpu.HBM))
+    )(peer, *prepared, pltpu.with_memory_space_constraint(jnp.asarray(inverse_table()), pltpu.HBM))
     parts = lax.all_to_all(partial.reshape(width, 4, HALF), ("row", "col"), split_axis=0, concat_axis=0, tiled=True)
     return pl.pallas_call(
         owner_kernel,

time: 29.3 us -> 29.2 us (level)
  no operation moved by 1% of the time
where the time goes in v5:
time: 29.2 us; the launch traced here: 29.1 us
  blocking collectives  21.5 us (74%)
  Pallas kernels  6.11 us (21%)
  starting transfers between devices  1.42 us (5%)
    all_to_all x1, blocking collectives, per_device(): lax.all_to_all(partial.reshape(width, 4, HALF), ('row', 'col'), split_axi...  21.5 us
    pallas_call x1, Pallas kernels, per_device(): pl.pallas_call(stack_kernel, out_shape=[jax.ShapeDtypeStruct((4 * width,...  3.69 us
    pallas_call x1, Pallas kernels, per_device(): pl.pallas_call(own_kernel, out_shape=[jax.ShapeDtypeStruct((8 * HALF, wid...  1.6 us
    ppermute x1, starting transfers between devices, per_device(): peer = lax.ppermute(volts, 'row', swap)  1.42 us
    pallas_call x1, Pallas kernels, per_device(): pl.pallas_call(owner_kernel, out_shape=jax.ShapeDtypeStruct((2, 2 * CHAN,...  0.82 us
  transfers between devices with their start and end apart: 1, of which 0 were waited for; matrix products, arithmetic and copies ran while one was open for 0% of the time, Pallas kernels for 6%

profile of v5, /device:TPU:1, one launch (start us, length us, event | category | flops | bytes accessed | tf_op | source)
XLA Modules:
  0.0 29.1 jit_solution(16601214007639331750)
XLA Ops:
  0.0 1.4 %collective-permute-start = (bf16[2,4,16384]{2,1,0:T(4,128)(2,1)}, bf16[2,4,16384]{2,1,0:T(4,128)(2,1)S(1)}, u32[]{:S(2)}, u32[]{:S(2)}) collective-permute-start(bf16[2,4,16384]{2,1,0:T(4,128)(2,1)} %own_hbm.1), channel_id=1, source_target_pairs={{0,16},{16,0},{32,48},{48,32},{64,80},{80,64},{96,112},{112,96},{1... | collective-permute-start | bytes 786440 | tf_op jit(solution)/shard_map/ppermute | solution.py:247
  1.4 1.6 %own_kernel.1 = (f32[1024,128]{1,0:T(8,128)S(1)}, f32[2,128,128]{2,1,0:T(8,128)S(1)}, bf16[512,512]{1,0:T(8,128)(2,1)S(1)}, bf16[256,256]{1,0:T(8,128)(2,1)S(1)}, f32[2,256]{1,0:T(2,128)S(1)}) custom-call(s32[1]{0:T(128)} %bitcast.core_ref, s32[1]{0:T(128)} %bitcast.1.device_ref, bf16[2,4,16384]{2,1,0:T(4,128)(2,1)} %own_hbm.1, ...), custom_call_target="tpu_custom_call" | custom-call | tf_op jit(solution)/shard_map/own_kernel/pallas_call | solution.py:252
  3.0 0.0 collective-permute-done.peer_ref
  3.0 3.7 %stack_kernel.1 = (f32[512,128]{1,0:T(8,128)S(1)}, bf16[2,256,256]{2,1,0:T(8,128)(2,1)S(1)}) custom-call(bf16[2,4,16384]{2,1,0:T(4,128)(2,1)S(1)} %collective-permute-done.peer_ref, f32[1024,128]{1,0:T(8,128)S(1)} %get-tuple-element.12.own_bins_ref, f32[2,128,128]{2,1,0:T(8,128)S(1)} %get-tuple-element.13.mask_ref, ...), custom_call_target="tpu_custom_call" | custom-call | tf_op jit(solution)/shard_map/stack_kernel/pallas_call | solution.py:276
  6.7 21.5 %all_to_all.5.parts_ref = f32[128,4,128]{2,1,0:T(4,128)S(1)} all-to-all(f32[128,4,128]{2,1,0:T(4,128)S(1)} %bitcast.4), channel_id=1, replica_groups=mesh['row'=8,'col'=16] {'row','col'}, dimensions={0} | all-to-all | bytes 524288 | tf_op jit(solution)/shard_map/all_to_all | solution.py:293
  28.2 0.8 %owner_kernel.1 = f32[2,4,255]{2,1,0:T(4,128)} custom-call(f32[128,4,128]{2,1,0:T(4,128)S(1)} %all_to_all.5.parts_ref, bf16[2,256,256]{2,1,0:T(8,128)(2,1)S(1)} %get-tuple-element.17.table_ref, f32[2,256]{1,0:T(2,128)S(1)} %get-tuple-element.18.scale_ref), custom_call_target="tpu_custom_call" | custom-call | tf_op jit(solution)/shard_map/owner_kernel/pallas_call | solution.py:294
Async XLA Ops:
  0.0 3.0 %collective-permute-start = (bf16[2,4,16384]{2,1,0:T(4,128)(2,1)}, bf16[2,4,16384]{2,1,0:T(4,128)(2,1)S(1)}, u32[]{:S(2)}, u32[]{:S(2)}) collective-permute-start(bf16[2,4,16384]{2,1,0:T(4,128)(2,1)} %own_hbm.1), channel_id=1, source_target_pairs={{0,16},{16,0},{32,48},{48,32},{64,80},{80,64},{96,112},{112,96},{1... | collective-permute-start | bytes 786440 | tf_op jit(solution)/shard_map/ppermute | solution.py:247
